TPU v7x, 512 devices: a whole 4x4x16 slice. The times are simulated.
512 devices in a mesh: wide: 64 (over y, z_hi, x, core), narrow: 8 (over z_lo).
Axes of the slice: x: 4, y: 4, z: 16 (z_hi: 2, z_lo: 8; z = z_hi * 8 + z_lo), core: 2. Of those that a mesh axis runs over, the one named last changes fastest.
Arguments:
- spectra: bfloat16 [384, 2, 2, 4096], P('wide', None, None, 'narrow'), may hold values from -6 to 6
- dead_mask: int32 [384], P('wide'), may hold values 0 or 1
- seg_offsets: int32 [384, 2], P('wide'), may hold values from 0 to 32767
- src_index: int32 [256], replicated, may hold values from 0 to 383, as said below
Outputs:
- correlations: float32 [256, 384, 512], P('narrow', 'wide')
Inputs may be any that keep to these rules, and one draw needn't show every extreme that they name: `src_index`: source j is one of the 6 channels j // 4 * 6 to j // 4 * 6 + 5; the 4 sources of one block are distinct; source 0 is channel 0 and source 256 - 4 is channel 384 - 1.
All inputs are finite; a program needn't handle non-finite values. No bound on the sum of `dead_mask` on one device may be relied on, other than what follows from the above.
Results may differ from a plain program's by a relative error of at most 0.0013.
Values may be sent and summed in bfloat16 or wider, within the bound.
No kernel may reach another device: no remote copies, remote signals or barrier semaphores. Data moves between devices by JAX's collectives and lax.ppermute only.
A program may use at most 128 MiB of HBM per device.

v0:
```python
import math

import jax
import jax.numpy as jnp
from jax import lax
from jax.sharding import PartitionSpec as P

NSAMP = 32768
LAGS = 512
SMOOTH = 64


EPSILON = 1e-06


def padded_2(cells, sides, width):
    for axis, dim in sides:
        count = lax.axis_size(axis)
        ends = count - 1
        head = lax.slice_in_dim(cells, 0, width, axis=dim)
        tail = lax.slice_in_dim(cells, cells.shape[dim] - width, cells.shape[dim], axis=dim)
        cells = jnp.concatenate(
            [
                lax.ppermute(tail, axis, [(i, (i + 1) % count) for i in range(ends)]),
                cells,
                lax.ppermute(head, axis, [((i + 1) % count, i) for i in range(ends)]),
            ],
            axis=dim,
        )
    return cells


def lag_table(first, length, lag_count):
    bins = first + jnp.arange(length, dtype=jnp.int32) + 1
    lag_steps = jnp.arange(lag_count, dtype=jnp.int32) - lag_count // 2 + NSAMP
    residue = bins[:, None] * lag_steps[None, :] % NSAMP
    angles = 2.0 * math.pi / NSAMP * residue.astype(jnp.float32)
    return jnp.concatenate([jnp.cos(angles), -jnp.sin(angles)], axis=0).astype(jnp.bfloat16)


def apply_whitening(real_part, imag_part, windowed, freq_bins, total_bins, dead_mask, seg_offsets):
    counts = (
        jnp.minimum(freq_bins + SMOOTH, total_bins - 1) - jnp.maximum(freq_bins - SMOOTH, 0) + 1
    ).astype(jnp.float32)
    smoothed = windowed / counts + EPSILON
    residue = (freq_bins + 1)[None, None, :] * seg_offsets[:, :, None] % NSAMP
    phase = 2.0 * math.pi / NSAMP * residue.astype(jnp.float32)
    scale = dead_mask.astype(jnp.float32)[:, None, None] / smoothed
    cosine = jnp.cos(phase)
    sine = jnp.sin(phase)
    white_real = (real_part * cosine - imag_part * sine) * scale
    white_imag = (real_part * sine + imag_part * cosine) * scale
    return jnp.stack([white_real, white_imag], axis=2).astype(jnp.bfloat16)


def cross_spectra(channels, sources, seg_count):
    chan_real = channels[:, :, 0]
    chan_imag = channels[:, :, 1]
    src_real = sources[:, :, 0]
    src_imag = sources[:, :, 1]
    cross_real = jnp.einsum(
        "ckf,skf->scf", chan_real, src_real, preferred_element_type=jnp.float32
    ) + jnp.einsum("ckf,skf->scf", chan_imag, src_imag, preferred_element_type=jnp.float32)
    cross_imag = jnp.einsum(
        "ckf,skf->scf", chan_imag, src_real, preferred_element_type=jnp.float32
    ) - jnp.einsum("ckf,skf->scf", chan_real, src_imag, preferred_element_type=jnp.float32)
    joined = jnp.concatenate([cross_real, cross_imag], axis=-1) * (1.0 / math.sqrt(seg_count))
    return joined.astype(jnp.bfloat16)


def body(spectra, dead_mask, seg_offsets, src_index):
    ch_count = spectra.shape[0]
    seg_count = spectra.shape[1]
    slice_bins = spectra.shape[3]
    narrow_count = lax.axis_size("narrow")
    wide_count = lax.axis_size("wide")
    total_bins = slice_bins * narrow_count
    narrow_pos = lax.axis_index("narrow")
    wide_pos = lax.axis_index("wide")
    freq_bins = narrow_pos * slice_bins + jnp.arange(slice_bins, dtype=jnp.int32)
    real_part = spectra[:, :, 0].astype(jnp.float32)
    imag_part = spectra[:, :, 1].astype(jnp.float32)
    amplitude = jnp.sqrt(real_part * real_part + imag_part * imag_part)
    padded = padded_2(amplitude, (("narrow", 2),), SMOOTH)
    windowed = lax.reduce_window(
        padded, jnp.zeros((), padded.dtype), lax.add, (1, 1, 2 * SMOOTH + 1), (1, 1, 1), "VALID"
    )
    whitened = apply_whitening(
        real_part, imag_part, windowed, freq_bins, total_bins, dead_mask, seg_offsets
    )
    per_block = src_index.shape[0] // wide_count
    own_rows = (
        lax.dynamic_slice_in_dim(src_index, wide_pos * per_block, per_block) - wide_pos * ch_count
    )
    selector = (own_rows[:, None] == jnp.arange(ch_count, dtype=jnp.int32)[None, :]).astype(
        jnp.bfloat16
    )
    chosen = jnp.einsum(
        "rc,ckqf->rkqf", selector, whitened, preferred_element_type=jnp.float32
    ).astype(jnp.bfloat16)
    share_rows = src_index.shape[0] // narrow_count
    norm_factor = 1.0 / math.sqrt(total_bins)
    panel = lax.all_gather(chosen, "wide", axis=0, tiled=True)
    table_part = lag_table(narrow_pos * slice_bins, slice_bins, LAGS)
    block = lax.slice_in_dim(panel, 0, share_rows * lax.axis_size("narrow"), axis=0)
    spectra_x = cross_spectra(whitened, block, seg_count)
    flat = spectra_x.reshape(share_rows * lax.axis_size("narrow") * ch_count, 2 * slice_bins)
    product = jnp.dot(flat, table_part, preferred_element_type=jnp.float32) * norm_factor
    return lax.psum_scatter(
        product.reshape(share_rows * lax.axis_size("narrow"), ch_count, LAGS),
        "narrow",
        scatter_dimension=0,
        tiled=True,
    )


def solution(mesh):
    placed = (P("wide", None, None, "narrow"), P("wide"), P("wide", None), P())
    return jax.shard_map(
        body, mesh=mesh, in_specs=placed, out_specs=P("narrow", "wide", None), check_vma=False
    )
```

profile of v0, /device:TPU:1, one launch (start us, length us, event | category | flops | bytes accessed | tf_op | source)
XLA Modules:
  0.0 386.9 jit_solution(2174678668443636968)
XLA Ops:
  6.5 0.0 all-gather.2.cloned.1.call-start
  6.5 0.9 fusion.44
  7.4 0.1 fusion.43
  7.5 4.4 %collective-permute-start = (f32[6,2,64]{2,0,1:T(8,128)S(1)}, f32[6,2,64]{2,0,1:T(8,128)S(1)}, u32[]{:S(2)}, u32[]{:S(2)}) collective-permute-start(f32[6,2,64]{2,0,1:T(8,128)S(1)} %get-tuple-element.9), channel_id=1, source_target_pairs={{0,1},{1,2},{2,3},{3,4},{4,5},{5,6},{6,7},{8,9},{9,10},{10,11},{11... | collective-permute-start | bytes 9224 | tf_op jit(solution)/shard_map/ppermute | solution.py:24
  11.9 1.3 collective-permute-start.1
  13.2 0.8 dynamic-slice_subtract_fusion
  14.0 0.7 convert_element_type.52
  14.6 0.0 collective-permute-done
  14.6 1.8 collective-permute-done.1
  16.5 0.1 maximum_bitcast_fusion
  16.6 107.8 %reduce_window.10 = f32[6,2,1,512]{3,2,1,0:T(1,128)S(1)} reduce-window(f32[6,2,1,640]{3,2,1,0:T(1,128)S(1)} %copy.35, f32[]{:T(128)} %constant.58.clone.1), window={size=1x1x1x129}, to_apply=%region_0.0 | reduce-window | flops 786432 | bytes 55300 | tf_op jit(solution)/shard_map/reduce_window | solution.py:85
  124.3 0.9 fusion.17
  125.2 0.2 convolution_convert_fusion
  125.4 0.6 copy.37
  126.1 0.0 all-gather.2.cloned.1.call-update
  126.1 0.2 reduce-scatter.2.cloned.1.call-start
  126.3 5.7 %cosine_convert_fusion = (bf16[512,512]{1,0:T(8,128)(2,1)}, bf16[512,512]{1,0:T(8,128)(2,1)}) fusion(s32[512]{0:T(512)S(1)} %iota_add_fusion, s32[512]{0:T(512)S(1)} %get-tuple-element.16), kind=kLoop, calls=%fused_computation.19 | loop fusion | flops 4456448 | bytes 1052672 | tf_op jit(solution)/shard_map/convert
  132.1 0.2 copy.39
  132.3 0.9 copy.41
  133.2 101.8 %all-gather.2.cloned.1.call-done = bf16[256,2,2,512]{3,2,1,0:T(2,128)(2,1)} async-done(((bf16[4,2,2,512]{3,2,1,0:T(2,128)(2,1)}), bf16[256,2,2,512]{3,2,1,0:T(2,128)(2,1)}) %all-gather.2.cloned.1.call-update) | async-done | bytes 1048592 | tf_op jit(solution)/shard_map/all_gather | solution.py:103
  235.0 3.3 fusion.42
  238.3 1.4 copy.50
  239.7 1.4 copy.51
  241.1 0.0 copy-start.1
  241.2 0.8 fusion.13
  242.0 3.7 fusion.11
  245.7 0.0 copy-done.1
  245.7 2.9 add_bitcast_fusion
  248.6 5.6 %copy.42 = f32[256,6,512]{2,1,0:T(8,128)} copy(f32[256,6,512]{0,1,2:T(8,128)} %add_bitcast_fusion) | data formatting | bytes 6291456 | tf_op jit(solution)/shard_map/add | solution.py:61
  254.2 4.7 %concatenate.16 = f32[1536,512]{1,0:T(8,128)} reshape(f32[256,6,512]{2,1,0:T(8,128)} %copy.42) | data formatting | bytes 6291456 | tf_op jit(solution)/shard_map/concatenate | solution.py:67
  258.9 5.1 %subtract_bitcast_fusion = f32[256,6,512]{0,1,2:T(8,128)} fusion(f32[512,256,6]{1,2,0:T(8,128)} %fusion.11, bf16[6,2,512]{0,1,2:T(2,128)(2,1)S(1)} %copy.39, bf16[256,2,1,512]{0,1,3,2:T(2,128)(2,1)S(1)} %copy.51), kind=kOutput, calls=%fused_computation.2 | convolution fusion | flops 3932160 | bytes 6828032 | tf_op jit(solution)/shard_map/ckf,skf->scf/dot_general | solution.py:66
  263.9 5.6 %copy.45 = f32[256,6,512]{2,1,0:T(8,128)} copy(f32[256,6,512]{0,1,2:T(8,128)} %subtract_bitcast_fusion) | data formatting | bytes 6291456 | tf_op jit(solution)/shard_map/sub | solution.py:64
  269.5 0.0 copy-start
  269.5 4.9 %concatenate.17 = f32[1536,512]{1,0:T(8,128)} reshape(f32[256,6,512]{2,1,0:T(8,128)} %copy.45) | data formatting | bytes 6291456 | tf_op jit(solution)/shard_map/concatenate | solution.py:67
  274.5 0.0 copy-done
  274.5 5.6 %convolution_multiply_fusion = f32[1536,512]{1,0:T(8,128)} fusion(f32[1536,512]{1,0:T(8,128)} %concatenate.17, f32[1536,512]{1,0:T(8,128)S(1)} %copy-done, bf16[512,512]{1,0:T(8,128)(2,1)} %get-tuple-element.14, bf16[512,512]{1,0:T(8,128)(2,1)} %get-tuple-element.13), kind=kOutput, calls=%fused_computation.4 | convolution fusion | flops 1618214912 | bytes 10485760 | tf_op jit(solution)/shard_map/dot_general | solution.py:108
  280.1 4.6 %reshape.101 = f32[256,6,512]{2,1,0:T(8,128)} reshape(f32[1536,512]{1,0:T(8,128)} %convolution_multiply_fusion) | data formatting | bytes 6291456 | tf_op jit(solution)/shard_map/reshape | solution.py:110
  284.6 0.0 reduce-scatter.2.cloned.1.call-update
  284.7 93.4 %reduce-scatter.2.cloned.1.call-done = f32[32,6,512]{2,1,0:T(8,128)} async-done(((f32[256,6,512]{2,1,0:T(8,128)}), f32[32,6,512]{2,1,0:T(8,128)}) %reduce-scatter.2.cloned.1.call-update) | async-done | bytes 393232 | tf_op jit(solution)/shard_map/reduce_scatter | solution.py:109
  378.1 2.0 copy.46
  (4 shorter events, 0.1 us)
Async XLA Ops:
  6.5 228.5 %all-gather.2.cloned.1.call-start = ((), (), s32[]{:S(2)}) async-start(), calls=%async_computation.1 | async-start | bytes 1064960 | tf_op jit(solution)/shard_map/all_gather | solution.py:103
  7.5 7.1 %collective-permute-start = (f32[6,2,64]{2,0,1:T(8,128)S(1)}, f32[6,2,64]{2,0,1:T(8,128)S(1)}, u32[]{:S(2)}, u32[]{:S(2)}) collective-permute-start(f32[6,2,64]{2,0,1:T(8,128)S(1)} %get-tuple-element.9), channel_id=1, source_target_pairs={{0,1},{1,2},{2,3},{3,4},{4,5},{5,6},{6,7},{8,9},{9,10},{10,11},{11... | collective-permute-start | bytes 9224 | tf_op jit(solution)/shard_map/ppermute | solution.py:24
  11.9 4.6 %collective-permute-start.1 = (f32[6,2,64]{2,0,1:T(8,128)S(1)}, f32[6,2,64]{2,0,1:T(8,128)S(1)}, u32[]{:S(2)}, u32[]{:S(2)}) collective-permute-start(f32[6,2,64]{2,0,1:T(8,128)S(1)} %get-tuple-element.10), channel_id=1, source_target_pairs={{1,0},{2,1},{3,2},{4,3},{5,4},{6,5},{7,6},{9,8},{10,9},{11,10},{12... | collective-permute-start | bytes 9224 | tf_op jit(solution)/shard_map/ppermute | solution.py:26
  126.1 252.0 %reduce-scatter.2.cloned.1.call-start = ((), (), s32[]{:S(2)}) async-start(), calls=%async_computation.2 | async-start | bytes 4718592 | tf_op jit(solution)/shard_map/reduce_scatter | solution.py:109
  241.1 4.5 %copy-start.1 = (bf16[6,2,512]{0,1,2:T(2,128)(2,1)S(1)}, bf16[6,2,512]{0,1,2:T(2,128)(2,1)}, u32[]{:S(2)}) copy-start(bf16[6,2,512]{0,1,2:T(2,128)(2,1)} %copy.41) | copy-start | bytes 36868
  269.5 4.9 %copy-start = (f32[1536,512]{1,0:T(8,128)S(1)}, f32[1536,512]{1,0:T(8,128)}, u32[]{:S(2)}) copy-start(f32[1536,512]{1,0:T(8,128)} %concatenate.16) | copy-start | bytes 9437188
Sparse Core Ops, SparseCore 0:
  126.2 108.7 all-gather.1
  284.8 93.2 reduce-scatter.1
where the time goes:
time: 388 us; the launch traced here: 387 us
  waiting for transfers between devices  197 us (51%)
  other arithmetic  116 us (30%)
  local copies, waits for them, and re-layouts  36.2 us (9%)
  matrix products  18.3 us (5%)
  between operations  13.5 us (3%)
  starting transfers between devices  5.88 us (2%)
    another operation x2, other arithmetic, body(): lax.reduce_window(padded, jnp.zeros((), padded.dtype), lax.add, (1, 1, 2...  108 us
    all_gather x1, waiting for transfers between devices, body(): panel = lax.all_gather(chosen, 'wide', axis=0, tiled=True)  102 us
    reduce_scatter x1, waiting for transfers between devices, body(): lax.psum_scatter(product.reshape(share_rows * lax.axis_size('narrow'), ch...  93.4 us
    concatenate x2, local copies, waits for them, and re-layouts, cross_spectra(): jnp.concatenate([cross_real, cross_imag], axis=-1)  9.59 us
  transfers between devices with their start and end apart: 4, of which 3 were waited for; matrix products, arithmetic and copies ran while one was open for 2% of the time, Pallas kernels for 0%

commit v1 on v0

v1 whole, which is shorter than its diff:
```python
import math

import jax
import jax.numpy as jnp
from jax import lax
from jax.experimental import pallas as pl
from jax.experimental.pallas import tpu as pltpu
from jax.sharding import Mesh, PartitionSpec as P

NSAMP = 32768
LAGS = 512
SMOOTH = 64
EPSILON = 1e-06
FREQS = 4096
SLICE = 512
CH = 6
SG = 4
SEGS = 2
LANES = 128


def unit_circle(residue):
    quarter = NSAMP // 4
    quadrant = (residue + quarter // 2) >> 13
    rest = (residue - quadrant * quarter).astype(jnp.float32) * (2.0 * math.pi / NSAMP)
    sq = rest * rest
    sine = rest * (1.0 + sq * (-1.0 / 6 + sq * (1.0 / 120 + sq * (-1.0 / 5040))))
    cosine = 1.0 + sq * (-0.5 + sq * (1.0 / 24 + sq * (-1.0 / 720 + sq * (1.0 / 40320))))
    swap = (quadrant & 1) == 1
    first = jnp.where(swap, sine, cosine)
    second = jnp.where(swap, cosine, sine)
    first = jnp.where(((quadrant + 1) & 2) == 2, -first, first)
    second = jnp.where((quadrant & 2) == 2, -second, second)
    return first, second


def whiten(real, imag, offsets):
    rows = real.shape[0]
    amplitude = jnp.sqrt(real * real + imag * imag)
    edge = jnp.zeros((rows, LANES), jnp.float32)
    padded = jnp.concatenate([edge, amplitude, edge], axis=1)
    width = FREQS + 2 * LANES
    run = padded
    for step in (1, 2, 4, 8, 16, 32, 64):
        run = run + pltpu.roll(run, width - step, 1)
    windowed = pltpu.roll(run, SMOOTH, 1) + pltpu.roll(padded, width - SMOOTH, 1)
    windowed = windowed[:, LANES : LANES + FREQS]
    bins = lax.broadcasted_iota(jnp.int32, (rows, FREQS), 1)
    counts = jnp.minimum(bins + SMOOTH, FREQS - 1) - jnp.maximum(bins - SMOOTH, 0) + 1
    smoothed = windowed / counts.astype(jnp.float32) + EPSILON
    scale = 1.0 / smoothed
    cosine, sine = unit_circle(((bins + 1) * offsets) & (NSAMP - 1))
    white_real = (real * cosine - imag * sine) * scale
    white_imag = (real * sine + imag * cosine) * scale
    return white_real.astype(jnp.bfloat16), white_imag.astype(jnp.bfloat16)


def whiten_sources_kernel(pieces_ref, out_ref):
    parts = [pieces_ref[i] for i in range(FREQS // SLICE)]
    cells = jnp.concatenate([p[:, :SLICE] for p in parts], axis=1).astype(jnp.float32)
    codes = parts[0][:, SLICE : SLICE + LANES].astype(jnp.float32)
    offsets = (codes[0:8] * 256.0 + codes[8:16]).astype(jnp.int32)[:, 0:1]
    real, imag = whiten(cells[0:8], cells[8:16], offsets)
    both = jnp.concatenate([real, imag], axis=0)
    for i in range(out_ref.shape[0]):
        out_ref[i] = both


def whiten_channels_kernel(pieces_ref, offsets_ref, out_ref):
    rows = SEGS * CH
    cells = jnp.concatenate([pieces_ref[i] for i in range(FREQS // SLICE)], axis=1)
    cells = cells.astype(jnp.float32)
    real, imag = whiten(cells[0:rows], cells[rows : 2 * rows], offsets_ref[:, 0:1])
    factor = 1.0 / math.sqrt(SEGS)
    out_ref[0:rows] = real.astype(jnp.float32) * factor
    out_ref[rows : 2 * rows] = imag.astype(jnp.float32) * factor


TABLE_ROWS = 256


def table_kernel(after_ref, out_ref):
    first = pl.program_id(0) * TABLE_ROWS
    shape = (16, LAGS)
    bins = lax.broadcasted_iota(jnp.int32, shape, 0) + 1
    lags = lax.broadcasted_iota(jnp.int32, shape, 1) - LAGS // 2 + NSAMP

    def step(i, carry):
        at = pl.multiple_of(i * 16, 16)
        cosine, sine = unit_circle(((bins + (first + at)) * lags) & (NSAMP - 1))
        out_ref[0, pl.ds(at, 16), :] = cosine.astype(jnp.bfloat16)
        out_ref[1, pl.ds(at, 16), :] = (-sine).astype(jnp.bfloat16)
        return carry

    lax.fori_loop(0, TABLE_ROWS // 16, step, 0)


def halves_sum(first, second, low):
    return jnp.where(low, first, second) + pltpu.roll(jnp.where(low, second, first), 4, 0)


def correlate_kernel(core_ref, mine_ref, other_ref, chan_ref, table_ref, out_ref, cross_ref, sum_ref):
    step = pl.program_id(0)
    low = lax.broadcasted_iota(jnp.int32, (8, LANES), 0) < 4
    for block in range(SLICE // LANES):
        lanes = slice(block * LANES, (block + 1) * LANES)
        chan = []
        for c in range(CH):
            tiles = []
            for q in range(2):
                base = q * SEGS * CH
                one = chan_ref[base + c : base + c + 1, lanes]
                two = chan_ref[base + CH + c : base + CH + c + 1, lanes]
                tiles.append(
                    jnp.where(low, jnp.broadcast_to(one, (8, LANES)), jnp.broadcast_to(two, (8, LANES)))
                )
            chan.append(tiles)
        for half, src_ref in enumerate((mine_ref, other_ref)):
            sources = [src_ref[x, :, lanes].astype(jnp.float32) for x in range(4)]
            for c in range(CH):
                creal, cimag = chan[c]
                reals, imags = [], []
                for x in range(4):
                    sreal, simag = sources[x][0:8], sources[x][8:16]
                    reals.append(creal * sreal + cimag * simag)
                    imags.append(cimag * sreal - creal * simag)
                at = half * CH * 16 + c * 16
                for q, got in enumerate((reals, imags)):
                    rows = jnp.concatenate(
                        [halves_sum(got[0], got[1], low), halves_sum(got[2], got[3], low)], axis=0
                    )
                    cross_ref[q, at : at + 16, lanes] = rows.astype(jnp.bfloat16)
    total = jnp.dot(cross_ref[0], table_ref[0], preferred_element_type=jnp.float32)
    total += jnp.dot(cross_ref[1], table_ref[1], preferred_element_type=jnp.float32)

    @pl.when(step == 0)
    def _():
        sum_ref[...] = total

    @pl.when(step > 0)
    def _():
        sum_ref[...] += total

    @pl.when(step == pl.num_programs(0) - 1)
    def _():
        core = core_ref[0]
        for half in range(2):
            which = core if half == 0 else 1 - core
            for x in range(4):
                for r in range(SG):
                    for c in range(CH):
                        row = half * CH * 16 + c * 16 + x * 4 + r
                        out_ref[x * 8 + which * 4 + r, c : c + 1, :] = sum_ref[row : row + 1, :] * (
                            1.0 / math.sqrt(FREQS)
                        )


def body(spectra, dead_mask, seg_offsets, src_index):
    wide_pos = ((lax.axis_index("y") * 2 + lax.axis_index("h")) * 4 + lax.axis_index("x")) * 2
    wide_pos = wide_pos + lax.axis_index("c")
    alive = spectra * dead_mask.astype(jnp.bfloat16)[:, None, None, None]
    rows = jnp.transpose(alive, (2, 1, 0, 3))
    chan_raw = lax.all_gather(rows.reshape(2 * SEGS * CH, SLICE), "n")

    own = lax.dynamic_slice_in_dim(src_index, wide_pos * SG, SG) - wide_pos * CH
    picked = jnp.zeros((2, SEGS, SG, SLICE), jnp.bfloat16)
    offs = jnp.zeros((SEGS, SG), jnp.int32)
    for c in range(CH):
        hit = own == c
        picked = jnp.where(hit[None, None, :, None], rows[:, :, c : c + 1, :], picked)
        offs = jnp.where(hit[None, :], seg_offsets[c][:, None], offs)
    codes = jnp.stack([offs // 256, offs % 256]).astype(jnp.bfloat16)
    codes = jnp.broadcast_to(codes[..., None], (2, SEGS, SG, LANES))
    payload = jnp.concatenate([picked, codes], axis=-1).reshape(16, SLICE + LANES)

    spread = lax.all_to_all(jnp.broadcast_to(payload[None], (8, 16, SLICE + LANES)), ("y", "h"), 0, 0)
    pieces = lax.all_to_all(spread, "n", 0, 0)

    vmem = pl.BlockSpec(memory_space=pltpu.VMEM)
    white_src = pl.pallas_call(
        whiten_sources_kernel,
        out_shape=jax.ShapeDtypeStruct((4, 16, FREQS), jnp.bfloat16),
        in_specs=[vmem],
        out_specs=vmem,
        compiler_params=pltpu.CompilerParams(vmem_limit_bytes=32 * 2**20),
        name="whiten_sources",
    )(pieces)
    mine = lax.all_to_all(white_src, "x", 0, 0)
    other = lax.ppermute(mine, "c", [(0, 1), (1, 0)])

    table = pl.pallas_call(
        table_kernel,
        grid=(FREQS // TABLE_ROWS,),
        out_shape=jax.ShapeDtypeStruct((2, FREQS, LAGS), jnp.bfloat16),
        in_specs=[pl.BlockSpec((1, 16, LANES), lambda i: (0, 0, 0))],
        out_specs=pl.BlockSpec((2, TABLE_ROWS, LAGS), lambda i: (0, i, 0)),
        compiler_params=pltpu.CompilerParams(vmem_limit_bytes=32 * 2**20),
        cost_estimate=pl.CostEstimate(flops=60 * FREQS * LAGS, bytes_accessed=4 * FREQS * LAGS, transcendentals=0),
        name="lag_table",
    )(spread)

    offsets = jnp.broadcast_to(seg_offsets.T.reshape(SEGS * CH, 1), (SEGS * CH, LANES))
    white_ch = pl.pallas_call(
        whiten_channels_kernel,
        out_shape=jax.ShapeDtypeStruct((2 * SEGS * CH, FREQS), jnp.float32),
        in_specs=[vmem, vmem],
        out_specs=vmem,
        compiler_params=pltpu.CompilerParams(vmem_limit_bytes=32 * 2**20),
        name="whiten_channels",
    )(chan_raw, offsets)

    core = lax.axis_index("c").astype(jnp.int32).reshape(1)
    return pl.pallas_call(
        correlate_kernel,
        grid=(FREQS // SLICE,),
        out_shape=jax.ShapeDtypeStruct((32, CH, LAGS), jnp.float32),
        in_specs=[
            pl.BlockSpec(memory_space=pltpu.SMEM),
            pl.BlockSpec((4, 16, SLICE), lambda i: (0, 0, i)),
            pl.BlockSpec((4, 16, SLICE), lambda i: (0, 0, i)),
            pl.BlockSpec((2 * SEGS * CH, SLICE), lambda i: (0, i)),
            pl.BlockSpec((2, SLICE, LAGS), lambda i: (0, i, 0)),
        ],
        out_specs=pl.BlockSpec((32, CH, LAGS), lambda i: (0, 0, 0)),
        scratch_shapes=[
            pltpu.VMEM((2, 2 * CH * 16, SLICE), jnp.bfloat16),
            pltpu.VMEM((2 * CH * 16, LAGS), jnp.float32),
        ],
        compiler_params=pltpu.CompilerParams(vmem_limit_bytes=40 * 2**20),
        name="correlate",
    )(core, mine, other, white_ch, table)


def solution(mesh):
    parts = Mesh(mesh.devices.reshape(4, 2, 4, 2, 8), ("y", "h", "x", "c", "n"))
    wide = ("y", "h", "x", "c")
    placed = (P(wide, None, None, "n"), P(wide), P(wide, None), P())
    return jax.shard_map(
        body, mesh=parts, in_specs=placed, out_specs=P("n", wide, None), check_vma=False
    )
```

time: 388 us -> 141 us (0.36)
  the two profiles are of different devices: /device:TPU:1 before, /device:TPU:2 now
where the time goes in v1:
time: 141 us
  blocking collectives  112 us (79%)
  Pallas kernels  20.7 us (15%)
  local copies, waits for them, and re-layouts  3.91 us (3%)
  other arithmetic  2.45 us (2%)
  starting transfers between devices  1.91 us (1%)
    all_gather x1, blocking collectives, body(): chan_raw = lax.all_gather(rows.reshape(2 * SEGS * CH, SLICE), 'n')  46.7 us
    all_to_all x1, blocking collectives, body(): lax.all_to_all(jnp.broadcast_to(payload[None], (8, 16, SLICE + LANES)), (...  33.4 us
    all_to_all x1, blocking collectives, body(): pieces = lax.all_to_all(spread, 'n', 0, 0)  20.4 us
    pallas_call x1, Pallas kernels, body(): pl.pallas_call(table_kernel, grid=(FREQS // TABLE_ROWS,), out_shape=jax.S...  13.3 us
    all_to_all x1, blocking collectives, body(): mine = lax.all_to_all(white_src, 'x', 0, 0)  11.3 us
    pallas_call x1, Pallas kernels, body(): pl.pallas_call(correlate_kernel, grid=(FREQS // SLICE,), out_shape=jax.Sh...  5.53 us
  transfers between devices with their start and end apart: 1, of which 0 were waited for; matrix products, arithmetic and copies ran while one was open for 1% of the time, Pallas kernels for 10%

profile of v1, /device:TPU:2, one launch (start us, length us, event | category | flops | bytes accessed | tf_op | source)
XLA Modules:
  0.0 141.1 jit_solution(9361836735901717910)
XLA Ops:
  0.0 0.7 convert_element_type.11
  0.7 0.8 broadcast_compare_fusion.7
  1.4 0.1 broadcast_in_dim.217
  1.5 0.1 broadcast_in_dim.223
  1.6 0.1 broadcast_in_dim.241
  1.7 0.1 broadcast_in_dim.235
  1.8 0.1 broadcast_in_dim.229
  1.9 0.1 broadcast_in_dim.247
  2.0 1.2 slice_reduce_fusion
  3.2 0.1 fusion.1
  3.3 0.1 convert_element_type.12
  3.4 0.8 multiply_bitcast_fusion
  4.5 0.1 select_select_fusion
  4.6 0.1 broadcast_in_dim.265
  4.7 33.4 %all_to_all.15.after_ref = bf16[8,16,640]{2,1,0:T(8,128)(2,1)S(1)} all-to-all(bf16[8,16,640]{2,1,0:T(8,128)(2,1)S(1)} %broadcast_in_dim.267), channel_id=1, replica_groups=mesh['y'=4,'h'=2,'x'=4,'c'=2,'n'=8] {'y','h'}, dimensions={0} | all-to-all | bytes 327680 | tf_op jit(solution)/shard_map/all_to_all | solution.py:176
  38.1 20.4 %all_to_all.16.pieces_ref = bf16[8,16,640]{2,1,0:T(8,128)(2,1)S(1)} all-to-all(bf16[8,16,640]{2,1,0:T(8,128)(2,1)S(1)} %all_to_all.15.after_ref), channel_id=1, replica_groups=mesh['y'=4,'h'=2,'x'=4,'c'=2,'n'=8] {'n'}, dimensions={0} | all-to-all | bytes 327680 | tf_op jit(solution)/shard_map/all_to_all | solution.py:177
  58.6 0.7 whiten_sources.1
  59.2 11.3 %all_to_all.17.mine_ref = bf16[4,16,4096]{2,1,0:T(8,128)(2,1)S(1)} all-to-all(bf16[4,16,4096]{2,1,0:T(8,128)(2,1)S(1)} %whiten_sources.1), channel_id=1, replica_groups=mesh['y'=4,'h'=2,'x'=4,'c'=2,'n'=8] {'x'}, dimensions={0} | all-to-all | bytes 1048576 | tf_op jit(solution)/shard_map/all_to_all | solution.py:188
  70.5 1.9 %collective-permute-start = (bf16[4,16,4096]{2,1,0:T(8,128)(2,1)S(1)}, bf16[4,16,4096]{2,1,0:T(8,128)(2,1)S(1)}, u32[]{:S(2)}, u32[]{:S(2)}) collective-permute-start(bf16[4,16,4096]{2,1,0:T(8,128)(2,1)S(1)} %all_to_all.17.mine_ref), channel_id=1, source_target_pairs={{0,8},{8,0},{1,9},{9,1},{2,10},{10,2},{3,11},{11,3},{4,12},{12,4},... | collective-permute-start | bytes 1572872 | tf_op jit(solution)/shard_map/ppermute | solution.py:189
  72.4 0.8 broadcast_in_dim.268
  73.2 46.7 %all_gather.3.pieces_ref = bf16[8,24,512]{2,1,0:T(8,128)(2,1)S(1)} all-gather(bf16[1,24,512]{2,1,0:T(8,128)(2,1)S(1)} %all_gather_reshape.3), channel_id=1, replica_groups=mesh['y'=4,'h'=2,'x'=4,'c'=2,'n'=8] {'n'}, dimensions={0}, use_global_device_ids=true | all-gather | bytes 221184 | tf_op jit(solution)/shard_map/all_gather | solution.py:163
  119.9 0.1 broadcast_in_dim.269.offsets_ref
  120.0 1.3 whiten_channels.1.chan_ref
  121.3 13.3 %lag_table.1.table_ref = bf16[2,4096,512]{2,1,0:T(8,128)(2,1)S(1)} custom-call(bf16[8,16,640]{2,1,0:T(8,128)(2,1)S(1)} %all_to_all.15.after_ref), custom_call_target="tpu_custom_call" | custom-call | flops 125829120 | bytes 8388608 | tf_op jit(solution)/shard_map/lag_table/pallas_call | solution.py:191
  134.6 0.0 collective-permute-done.other_ref
  134.6 5.5 %correlate.1 = f32[32,6,512]{2,1,0:T(8,128)S(1)} custom-call(s32[1]{0:T(128)} %bitcast.core_ref, bf16[4,16,4096]{2,1,0:T(8,128)(2,1)S(1)} %all_to_all.17.mine_ref, bf16[4,16,4096]{2,1,0:T(8,128)(2,1)S(1)} %collective-permute-done.other_ref, f32[24,4096]{1,0:T(8,128)S(1)} %whiten_channels.1.chan_ref, bf16[2,4096,512]{2,1,0:T(8,128)(2,1)S(1)} %lag_table.1.table_ref), custom_call_target="tpu_custom_call" | custom-call | tf_op jit(solution)/shard_map/correlate/pallas_call | solution.py:213
  140.1 1.0 copy.28
  (32 shorter events, 0.3 us)
Async XLA Ops:
  70.5 64.1 %collective-permute-start = (bf16[4,16,4096]{2,1,0:T(8,128)(2,1)S(1)}, bf16[4,16,4096]{2,1,0:T(8,128)(2,1)S(1)}, u32[]{:S(2)}, u32[]{:S(2)}) collective-permute-start(bf16[4,16,4096]{2,1,0:T(8,128)(2,1)S(1)} %all_to_all.17.mine_ref), channel_id=1, source_target_pairs={{0,8},{8,0},{1,9},{9,1},{2,10},{10,2},{3,11},{11,3},{4,12},{12,4},... | collective-permute-start | bytes 1572872 | tf_op jit(solution)/shard_map/ppermute | solution.py:189

commit v2 on v1

v2 whole, which is shorter than its diff:
```python
import math

import jax
import jax.numpy as jnp
from jax import lax
from jax.experimental import pallas as pl
from jax.experimental.pallas import tpu as pltpu
from jax.sharding import Mesh, PartitionSpec as P

NSAMP = 32768
LAGS = 512
SMOOTH = 64
EPSILON = 1e-06
FREQS = 4096
SLICE = 512
CH = 6
ROWS = 12
SG = 4
SEGS = 2
LANES = 128


def unit_circle(residue):
    quarter = NSAMP // 4
    quadrant = (residue + quarter // 2) >> 13
    rest = (residue - quadrant * quarter).astype(jnp.float32) * (2.0 * math.pi / NSAMP)
    sq = rest * rest
    sine = rest * (1.0 + sq * (-1.0 / 6 + sq * (1.0 / 120 + sq * (-1.0 / 5040))))
    cosine = 1.0 + sq * (-0.5 + sq * (1.0 / 24 + sq * (-1.0 / 720 + sq * (1.0 / 40320))))
    swap = (quadrant & 1) == 1
    first = jnp.where(swap, sine, cosine)
    second = jnp.where(swap, cosine, sine)
    first = jnp.where(((quadrant + 1) & 2) == 2, -first, first)
    second = jnp.where((quadrant & 2) == 2, -second, second)
    return first, second


def whiten_kernel(
    place_ref, mask_ref, offsets_ref, index_ref, before_ref, own_ref, after_ref, chan_ref, src_ref, keep_ref
):
    own = own_ref[...].astype(jnp.float32)
    before = before_ref[:, SLICE - LANES : SLICE].astype(jnp.float32)
    after = after_ref[:, 0:LANES].astype(jnp.float32)
    cells = jnp.concatenate([before, own, after], axis=1)
    real, imag = cells[0:ROWS], cells[ROWS : 2 * ROWS]
    width = SLICE + 2 * LANES
    amplitude = jnp.sqrt(real * real + imag * imag)
    run = amplitude
    for step in (1, 2, 4, 8, 16, 32, 64):
        run = run + pltpu.roll(run, width - step, 1)
    windowed = pltpu.roll(run, SMOOTH, 1) + pltpu.roll(amplitude, width - SMOOTH, 1)
    windowed = windowed[:, LANES : LANES + SLICE]
    real, imag = real[:, LANES : LANES + SLICE], imag[:, LANES : LANES + SLICE]

    row = lax.broadcasted_iota(jnp.int32, (ROWS, LANES), 0)
    offsets = jnp.zeros((ROWS, LANES), jnp.int32)
    alive = jnp.zeros((ROWS, LANES), jnp.int32)
    for k in range(SEGS):
        for c in range(CH):
            offsets = jnp.where(row == k * CH + c, offsets_ref[c, k], offsets)
            alive = jnp.where(row == k * CH + c, mask_ref[c], alive)
    alive = alive.astype(jnp.float32)
    bins = lax.broadcasted_iota(jnp.int32, (ROWS, SLICE), 1) + place_ref[1] * SLICE
    counts = jnp.minimum(bins + SMOOTH, FREQS - 1) - jnp.maximum(bins - SMOOTH, 0) + 1
    smoothed = windowed / counts.astype(jnp.float32) + EPSILON
    scale = jnp.concatenate([alive] * (SLICE // LANES), axis=1) / smoothed
    wide_offsets = jnp.concatenate([offsets] * (SLICE // LANES), axis=1)
    cosine, sine = unit_circle(((bins + 1) * wide_offsets) & (NSAMP - 1))
    keep_ref[0, 0:ROWS] = (real * cosine - imag * sine) * scale
    keep_ref[1, 0:ROWS] = (real * sine + imag * cosine) * scale

    both = jnp.concatenate([keep_ref[0, 0:ROWS], keep_ref[1, 0:ROWS]], axis=0).astype(jnp.bfloat16)
    for i in range(chan_ref.shape[0]):
        chan_ref[i] = both
    picked = []
    for q in range(2):
        for k in range(SEGS):
            for r in range(SG):
                at = index_ref[place_ref[0] * SG + r] - place_ref[0] * CH + k * CH
                picked.append(keep_ref[q, pl.ds(at, 1), :])
    src_ref[...] = jnp.concatenate(picked, axis=0).astype(jnp.bfloat16)


TABLE_STEPS = 16
INNER = 64


def table_kernel(after_ref, out_ref, inner_ref, outer_ref):
    lags = lax.broadcasted_iota(jnp.int32, (INNER, LAGS), 1) - LAGS // 2 + NSAMP
    row = lax.broadcasted_iota(jnp.int32, (INNER, LAGS), 0)

    @pl.when(pl.program_id(0) == 0)
    def _():
        cosine, sine = unit_circle(((row + 1) * lags) & (NSAMP - 1))
        inner_ref[0], inner_ref[1] = cosine, sine
        cosine, sine = unit_circle((row * INNER * lags) & (NSAMP - 1))
        outer_ref[0], outer_ref[1] = cosine, sine

    per_step = FREQS // INNER // TABLE_STEPS
    for j in range(per_step):
        at = pl.program_id(0) * per_step + j
        ocos, osin = outer_ref[0, pl.ds(at, 1), :], outer_ref[1, pl.ds(at, 1), :]
        for lane in range(LAGS // LANES):
            lanes = slice(lane * LANES, (lane + 1) * LANES)
            wcos = jnp.broadcast_to(ocos[:, lanes], (16, LANES))
            wsin = jnp.broadcast_to(osin[:, lanes], (16, LANES))
            for i in range(INNER // 16):
                rows = slice(i * 16, i * 16 + 16)
                icos, isin = inner_ref[0, rows, lanes], inner_ref[1, rows, lanes]
                put = slice(j * INNER + i * 16, j * INNER + i * 16 + 16)
                out_ref[0, put, lanes] = (icos * wcos - isin * wsin).astype(jnp.bfloat16)
                out_ref[1, put, lanes] = (-(isin * wcos + icos * wsin)).astype(jnp.bfloat16)


def halves_sum(first, second, low):
    return jnp.where(low, first, second) + pltpu.roll(jnp.where(low, second, first), 4, 0)


def correlate_kernel(
    place_ref, mine_ref, other_ref, chan_ref, table_ref, out_ref, wide_ref, cross_ref, sum_ref
):
    step = pl.program_id(0)
    low = lax.broadcasted_iota(jnp.int32, (8, LANES), 0) < 4
    wide_ref[...] = chan_ref[0].astype(jnp.float32) * (1.0 / math.sqrt(SEGS))
    for block in range(SLICE // LANES):
        lanes = slice(block * LANES, (block + 1) * LANES)
        chan = []
        for c in range(CH):
            tiles = []
            for q in range(2):
                base = q * ROWS
                one = wide_ref[base + c : base + c + 1, lanes]
                two = wide_ref[base + CH + c : base + CH + c + 1, lanes]
                tiles.append(
                    jnp.where(low, jnp.broadcast_to(one, (8, LANES)), jnp.broadcast_to(two, (8, LANES)))
                )
            chan.append(tiles)
        for half, src_ref in enumerate((mine_ref, other_ref)):
            sources = [src_ref[0, x, 0, :, lanes].astype(jnp.float32) for x in range(4)]
            for c in range(CH):
                creal, cimag = chan[c]
                reals, imags = [], []
                for x in range(4):
                    sreal, simag = sources[x][0:8], sources[x][8:16]
                    reals.append(creal * sreal + cimag * simag)
                    imags.append(cimag * sreal - creal * simag)
                at = half * CH * 16 + c * 16
                for q, got in enumerate((reals, imags)):
                    rows = jnp.concatenate(
                        [halves_sum(got[0], got[1], low), halves_sum(got[2], got[3], low)], axis=0
                    )
                    cross_ref[q, at : at + 16, lanes] = rows.astype(jnp.bfloat16)
    total = jnp.dot(cross_ref[0], table_ref[0], preferred_element_type=jnp.float32)
    total += jnp.dot(cross_ref[1], table_ref[1], preferred_element_type=jnp.float32)
    total = total.reshape(2, CH, 16, LAGS)

    @pl.when(step == 0)
    def _():
        sum_ref[...] = total

    @pl.when(step > 0)
    def _():
        sum_ref[...] += total

    @pl.when(step == pl.num_programs(0) - 1)
    def _():
        core = place_ref[1]
        for c in range(CH):
            zero, one = sum_ref[core, c], sum_ref[1 - core, c]
            for x in range(4):
                rows = slice(x * 4, x * 4 + 4)
                both = jnp.concatenate([zero[rows], one[rows]], axis=0)
                out_ref[c, x * 8 : x * 8 + 8, :] = both * (1.0 / math.sqrt(FREQS))


def transposed(flip):
    pairs = []
    for y in range(4):
        for h in range(2):
            for n in range(8):
                to_y, to_h, to_n = n // 2, (n % 2) ^ flip, 2 * y + h
                pairs.append(((y * 2 + h) * 8 + n, (to_y * 2 + to_h) * 8 + to_n))
    return pairs


def body(spectra, dead_mask, seg_offsets, src_index):
    pos = {axis: lax.axis_index(axis).astype(jnp.int32) for axis in ("y", "h", "x", "c", "n")}
    wide_pos = ((pos["y"] * 2 + pos["h"]) * 4 + pos["x"]) * 2 + pos["c"]
    rows = jnp.transpose(spectra, (2, 1, 0, 3)).reshape(2 * ROWS, SLICE)
    before = lax.ppermute(rows, "n", [(i, i + 1) for i in range(7)])
    after = lax.ppermute(rows, "n", [(i + 1, i) for i in range(7)])

    vmem = pl.BlockSpec(memory_space=pltpu.VMEM)
    smem = pl.BlockSpec(memory_space=pltpu.SMEM)
    chan_out, src_out = pl.pallas_call(
        whiten_kernel,
        out_shape=(
            jax.ShapeDtypeStruct((8, 2 * ROWS, SLICE), jnp.bfloat16),
            jax.ShapeDtypeStruct((16, SLICE), jnp.bfloat16),
        ),
        in_specs=[smem, smem, smem, smem, vmem, vmem, vmem],
        out_specs=(vmem, vmem),
        scratch_shapes=[pltpu.VMEM((2, 16, SLICE), jnp.float32)],
        compiler_params=pltpu.CompilerParams(vmem_limit_bytes=32 * 2**20),
        name="whiten",
    )(jnp.stack([wide_pos, pos["n"]]), dead_mask, seg_offsets, src_index, before, rows, after)

    moved = [lax.ppermute(src_out, ("y", "h", "n"), transposed(flip)) for flip in range(2)]
    chan_all = lax.all_to_all(chan_out, "n", 0, 0)
    pair = jnp.stack(moved)
    mine = lax.all_to_all(jnp.broadcast_to(pair[None], (16,) + pair.shape), ("y", "x"), 0, 0)
    mine = mine.reshape((4, 4) + pair.shape)
    other = lax.ppermute(mine, "c", [(0, 1), (1, 0)])

    table = pl.pallas_call(
        table_kernel,
        grid=(TABLE_STEPS,),
        out_shape=jax.ShapeDtypeStruct((2, FREQS, LAGS), jnp.bfloat16),
        in_specs=[pl.BlockSpec((16, LANES), lambda i: (0, 0))],
        out_specs=pl.BlockSpec((2, FREQS // TABLE_STEPS, LAGS), lambda i: (0, i, 0)),
        scratch_shapes=[pltpu.VMEM((2, INNER, LAGS), jnp.float32), pltpu.VMEM((2, FREQS // INNER, LAGS), jnp.float32)],
        compiler_params=pltpu.CompilerParams(vmem_limit_bytes=32 * 2**20),
        cost_estimate=pl.CostEstimate(flops=8 * FREQS * LAGS, bytes_accessed=4 * FREQS * LAGS, transcendentals=0),
        name="lag_table",
    )(src_out)

    def source_block(i, place):
        return (i // 2, 0, lax.rem(i + place[0], 2), 0, 0)

    src_spec = pl.BlockSpec((1, 4, 1, 16, SLICE), source_block)
    out = pl.pallas_call(
        correlate_kernel,
        grid_spec=pltpu.PrefetchScalarGridSpec(
            num_scalar_prefetch=1,
            grid=(FREQS // SLICE,),
            in_specs=[
                src_spec,
                src_spec,
                pl.BlockSpec((1, 2 * ROWS, SLICE), lambda i, place: (i, 0, 0)),
                pl.BlockSpec((2, SLICE, LAGS), lambda i, place: (0, i, 0)),
            ],
            out_specs=pl.BlockSpec((CH, 32, LAGS), lambda i, place: (0, 0, 0)),
            scratch_shapes=[
                pltpu.VMEM((2 * ROWS, SLICE), jnp.float32),
                pltpu.VMEM((2, 2 * CH * 16, SLICE), jnp.bfloat16),
                pltpu.VMEM((2, CH, 16, LAGS), jnp.float32),
            ],
        ),
        out_shape=jax.ShapeDtypeStruct((CH, 32, LAGS), jnp.float32),
        compiler_params=pltpu.CompilerParams(vmem_limit_bytes=40 * 2**20),
        name="correlate",
    )(jnp.stack([pos["h"], pos["c"]]), mine, other, chan_all, table)
    return jnp.transpose(out, (1, 0, 2))


def solution(mesh):
    parts = Mesh(mesh.devices.reshape(4, 2, 4, 2, 8), ("y", "h", "x", "c", "n"))
    wide = ("y", "h", "x", "c")
    placed = (P(wide, None, None, "n"), P(wide), P(wide, None), P())
    return jax.shard_map(
        body, mesh=parts, in_specs=placed, out_specs=P("n", wide, None), check_vma=False
    )
```

time: 141 us -> 82.3 us (0.58)
  blocking collectives: 112 us -> 27.1 us
  starting transfers between devices: 1.91 us -> 27.8 us
  Pallas kernels: 20.7 us -> 12.7 us
  local copies, waits for them, and re-layouts: 3.91 us -> 9.51 us
  waiting for transfers between devices: 0.01 us -> 4.55 us
  other arithmetic: 2.45 us -> 0.16 us
    all_gather x1 -> x0, blocking collectives: 46.7 us -> none  [body(): chan_raw = lax.all_gather(rows.reshape(2 * SEGS * CH, SLICE), 'n')]
    all_to_all x3 -> x1, blocking collectives: 65.1 us -> 27.1 us  [body(): lax.all_to_all(jnp.broadcast_to(pair[None], (16,) + pair.shape), ('y', 'x...]
    ppermute x0 -> x4, starting transfers between devices: none -> 22.2 us  [the longest x2 16.4 us: body(): lax.ppermute(src_out, ('y', 'h', 'n'), transposed(flip))]
    unnamed x0 -> x9, local copies, waits for them, and re-layouts: none -> 8.69 us
    pallas_call x4 -> x3, Pallas kernels: 20.7 us -> 12.7 us  [the longest x1 7.03 us: body(): pl.pallas_call(correlate_kernel, grid_spec=pltpu.PrefetchScalarGridSpec(n...]
    all_to_all x0 -> x1, starting transfers between devices: none -> 3.66 us  [body(): chan_all = lax.all_to_all(chan_out, 'n', 0, 0)]
    all_to_all x0 -> x1, waiting for transfers between devices: none -> 3.15 us  [body(): chan_all = lax.all_to_all(chan_out, 'n', 0, 0)]
    broadcast_in_dim x35 -> x1, local copies, waits for them, and re-layouts: 1.66 us -> 0.05 us  [body(): jnp.broadcast_to(pair[None], (16,) + pair.shape)]
  transfers between devices with their start and end apart: 1 -> 6, of which waited for: 0 -> 3; matrix products, arithmetic and copies ran while one was open for 1% -> 1% of each run, Pallas kernels for 10% -> 5%
where the time goes in v2:
time: 82.3 us; the launch traced here: 81.8 us
  starting transfers between devices  27.8 us (34%)
  blocking collectives  27.1 us (33%)
  Pallas kernels  12.7 us (15%)
  local copies, waits for them, and re-layouts  9.51 us (12%)
  waiting for transfers between devices  4.55 us (6%)
    all_to_all x1, blocking collectives, body(): lax.all_to_all(jnp.broadcast_to(pair[None], (16,) + pair.shape), ('y', 'x...  27.1 us
    ppermute x2, starting transfers between devices, body(): lax.ppermute(src_out, ('y', 'h', 'n'), transposed(flip))  16.4 us
    unnamed x9, local copies, waits for them, and re-layouts  8.69 us
    pallas_call x1, Pallas kernels, body(): pl.pallas_call(correlate_kernel, grid_spec=pltpu.PrefetchScalarGridSpec(n...  7.03 us
    ppermute x1, starting transfers between devices, body(): before = lax.ppermute(rows, 'n', [(i, i + 1) for i in range(7)])  4.55 us
    pallas_call x1, Pallas kernels, body(): pl.pallas_call(table_kernel, grid=(TABLE_STEPS,), out_shape=jax.ShapeDtyp...  3.73 us
    all_to_all x1, starting transfers between devices, body(): chan_all = lax.all_to_all(chan_out, 'n', 0, 0)  3.66 us
    all_to_all x1, waiting for transfers between devices, body(): chan_all = lax.all_to_all(chan_out, 'n', 0, 0)  3.15 us
  transfers between devices with their start and end apart: 6, of which 3 were waited for; matrix products, arithmetic and copies ran while one was open for 1% of the time, Pallas kernels for 5%

profile of v2, /device:TPU:2, one launch (start us, length us, event | category | flops | bytes accessed | tf_op | source)
XLA Modules:
  0.0 81.8 jit_solution(2355304410641393494)
XLA Ops:
  0.0 0.7 copy.7
  0.8 1.3 %collective-permute-start.1 = (bf16[24,512]{1,0:T(8,128)(2,1)S(1)}, bf16[24,512]{1,0:T(8,128)(2,1)S(1)}, u32[]{:S(2)}, u32[]{:S(2)}) collective-permute-start(bf16[24,512]{1,0:T(8,128)(2,1)S(1)} %reshape.7.own_ref), channel_id=1, source_target_pairs={{1,0},{2,1},{3,2},{4,3},{5,4},{6,5},{7,6},{9,8},{10,9},{11,10},{12... | collective-permute-start | bytes 73736 | tf_op jit(solution)/shard_map/ppermute | solution.py:191
  2.1 4.5 %collective-permute-start = (bf16[24,512]{1,0:T(8,128)(2,1)S(1)}, bf16[24,512]{1,0:T(8,128)(2,1)S(1)}, u32[]{:S(2)}, u32[]{:S(2)}) collective-permute-start(bf16[24,512]{1,0:T(8,128)(2,1)S(1)} %reshape.7.own_ref), channel_id=1, source_target_pairs={{0,1},{1,2},{2,3},{3,4},{4,5},{5,6},{6,7},{8,9},{9,10},{10,11},{11... | collective-permute-start | bytes 73736 | tf_op jit(solution)/shard_map/ppermute | solution.py:190
  6.6 0.1 pad_add_fusion.1.place_ref
  6.7 0.8 copy.8.offsets_ref
  7.5 0.0 collective-permute-done.1.after_ref
  7.5 0.6 collective-permute-done.before_ref
  8.1 0.0 copy-start.2
  8.1 0.7 copy-done.2
  8.8 0.0 copy-start.3
  8.8 0.7 copy-done.3
  9.5 1.9 %whiten.1 = (bf16[8,24,512]{2,1,0:T(8,128)(2,1)}, bf16[16,512]{1,0:T(8,128)(2,1)S(1)}) custom-call(s32[2]{0:T(128)S(1)} %pad_add_fusion.1.place_ref, s32[6]{0:T(128)S(1)} %copy-done.3, s32[6,2]{1,0:T(8,128)S(1)} %copy.8.offsets_ref, s32[256]{0:T(256)S(1)} %copy-done.2, bf16[24,512]{1,0:T(8,128)(2,1)S(1)} %collective-permute-done.before_ref, ...), custom_call_target="tpu_custom_call" | custom-call | tf_op jit(solution)/shard_map/whiten/pallas_call | solution.py:195
  11.4 15.7 %collective-permute-start.3 = (bf16[16,512]{1,0:T(8,128)(2,1)S(1)}, bf16[16,512]{1,0:T(8,128)(2,1)S(1)}, u32[]{:S(2)}, u32[]{:S(2)}) collective-permute-start(bf16[16,512]{1,0:T(8,128)(2,1)S(1)} %get-tuple-element.7.after_ref), channel_id=1, source_target_pairs={{0,64},{1,0},{2,192},{3,128},{4,320},{5,256},{6,448},{7,384},{64,6... | collective-permute-start | bytes 49160 | tf_op jit(solution)/shard_map/ppermute | solution.py:208
  27.1 0.7 collective-permute-start.2
  27.8 0.8 collective-permute-done.3
  28.5 0.0 collective-permute-done.2
  28.5 0.1 broadcast_in_dim.2
  28.6 27.1 %all_to_all.10 = bf16[16,2,16,512]{3,2,1,0:T(8,128)(2,1)S(1)} all-to-all(bf16[16,2,16,512]{3,2,1,0:T(8,128)(2,1)S(1)} %broadcast_in_dim.2), channel_id=1, replica_groups=mesh['y'=4,'h'=2,'x'=4,'c'=2,'n'=8] {'y','x'}, dimensions={0} | all-to-all | bytes 1048576 | tf_op jit(solution)/shard_map/all_to_all | solution.py:211
  55.7 3.7 %all-to-all-start.1 = ((bf16[8,24,512]{2,1,0:T(8,128)(2,1)}), bf16[8,24,512]{2,1,0:T(8,128)(2,1)S(1)}, u32[]{:S(2)}, u32[]{:S(2)}) async-start(bf16[8,24,512]{2,1,0:T(8,128)(2,1)} %get-tuple-element.8), calls=%async_computation.1 | async-start | bytes 393216 | tf_op jit(solution)/shard_map/all_to_all | solution.py:209
  59.3 1.9 %collective-permute-start.4 = (bf16[4,4,2,16,512]{4,3,2,1,0:T(8,128)(2,1)S(1)}, bf16[4,4,2,16,512]{4,3,2,1,0:T(8,128)(2,1)S(1)}, u32[]{:S(2)}, u32[]{:S(2)}) collective-permute-start(bf16[4,4,2,16,512]{4,3,2,1,0:T(8,128)(2,1)S(1)} %bitcast.9), channel_id=1, source_target_pairs={{0,8},{8,0},{1,9},{9,1},{2,10},{10,2},{3,11},{11,3},{4,12},{12,4},... | collective-permute-start | bytes 1572872 | tf_op jit(solution)/shard_map/ppermute | solution.py:213
  61.2 0.1 pad_add_fusion.place_ref
  61.3 3.7 %lag_table.1.table_ref = bf16[2,4096,512]{2,1,0:T(8,128)(2,1)S(1)} custom-call(bf16[16,512]{1,0:T(8,128)(2,1)S(1)} %get-tuple-element.7.after_ref), custom_call_target="tpu_custom_call" | custom-call | flops 16777216 | bytes 8388608 | tf_op jit(solution)/shard_map/lag_table/pallas_call | solution.py:215
  65.0 0.0 copy-start
  65.1 3.2 %copy-done = bf16[2,4096,512]{2,1,0:T(8,128)(2,1)} copy-done((bf16[2,4096,512]{2,1,0:T(8,128)(2,1)}, bf16[2,4096,512]{2,1,0:T(8,128)(2,1)S(1)}, u32[]{:S(2)}) %copy-start) | copy-done | bytes 8388632
  68.3 3.1 %all-to-all-done.1.chan_ref = bf16[8,24,512]{2,1,0:T(8,128)(2,1)S(1)} async-done(((bf16[8,24,512]{2,1,0:T(8,128)(2,1)}), bf16[8,24,512]{2,1,0:T(8,128)(2,1)S(1)}, u32[]{:S(2)}, u32[]{:S(2)}) %all-to-all-start.1) | async-done | bytes 196640 | tf_op jit(solution)/shard_map/all_to_all | solution.py:209
  71.4 0.0 collective-permute-done.4.other_ref
  71.4 0.0 copy-start.1
  71.4 3.4 %copy-done.1 = bf16[2,4096,512]{2,1,0:T(8,128)(2,1)S(1)} copy-done((bf16[2,4096,512]{2,1,0:T(8,128)(2,1)S(1)}, bf16[2,4096,512]{2,1,0:T(8,128)(2,1)}, u32[]{:S(2)}) %copy-start.1) | copy-done | bytes 8388632
  74.8 7.0 %correlate.1 = f32[6,32,512]{2,1,0:T(8,128)} custom-call(s32[2]{0:T(128)S(1)} %pad_add_fusion.place_ref, bf16[4,4,2,16,512]{4,3,2,1,0:T(8,128)(2,1)S(1)} %bitcast.10, bf16[4,4,2,16,512]{4,3,2,1,0:T(8,128)(2,1)S(1)} %collective-permute-done.4.other_ref, bf16[8,24,512]{2,1,0:T(8,128)(2,1)S(1)} %all-to-all-done.1.chan_ref, bf16[2,4096,512]{2,1,0:T(8,128)(2,1)S(1)} %copy-done.1), custom_call_target="tpu_custom_call" | custom-call | tf_op jit(solution)/shard_map/correlate/pallas_call | solution.py:231
  (2 shorter events, 0.0 us)
Async XLA Ops:
  0.8 6.7 %collective-permute-start.1 = (bf16[24,512]{1,0:T(8,128)(2,1)S(1)}, bf16[24,512]{1,0:T(8,128)(2,1)S(1)}, u32[]{:S(2)}, u32[]{:S(2)}) collective-permute-start(bf16[24,512]{1,0:T(8,128)(2,1)S(1)} %reshape.7.own_ref), channel_id=1, source_target_pairs={{1,0},{2,1},{3,2},{4,3},{5,4},{6,5},{7,6},{9,8},{10,9},{11,10},{12... | collective-permute-start | bytes 73736 | tf_op jit(solution)/shard_map/ppermute | solution.py:191
  2.1 6.1 %collective-permute-start = (bf16[24,512]{1,0:T(8,128)(2,1)S(1)}, bf16[24,512]{1,0:T(8,128)(2,1)S(1)}, u32[]{:S(2)}, u32[]{:S(2)}) collective-permute-start(bf16[24,512]{1,0:T(8,128)(2,1)S(1)} %reshape.7.own_ref), channel_id=1, source_target_pairs={{0,1},{1,2},{2,3},{3,4},{4,5},{5,6},{6,7},{8,9},{9,10},{10,11},{11... | collective-permute-start | bytes 73736 | tf_op jit(solution)/shard_map/ppermute | solution.py:190
  8.1 0.7 copy-start.2
  8.8 0.7 copy-start.3
  11.4 17.1 %collective-permute-start.3 = (bf16[16,512]{1,0:T(8,128)(2,1)S(1)}, bf16[16,512]{1,0:T(8,128)(2,1)S(1)}, u32[]{:S(2)}, u32[]{:S(2)}) collective-permute-start(bf16[16,512]{1,0:T(8,128)(2,1)S(1)} %get-tuple-element.7.after_ref), channel_id=1, source_target_pairs={{0,64},{1,0},{2,192},{3,128},{4,320},{5,256},{6,448},{7,384},{64,6... | collective-permute-start | bytes 49160 | tf_op jit(solution)/shard_map/ppermute | solution.py:208
  27.1 1.4 %collective-permute-start.2 = (bf16[16,512]{1,0:T(8,128)(2,1)S(1)}, bf16[16,512]{1,0:T(8,128)(2,1)S(1)}, u32[]{:S(2)}, u32[]{:S(2)}) collective-permute-start(bf16[16,512]{1,0:T(8,128)(2,1)S(1)} %get-tuple-element.7.after_ref), channel_id=1, source_target_pairs={{0,0},{1,64},{2,128},{3,192},{4,256},{5,320},{6,384},{7,448},{64,1... | collective-permute-start | bytes 49160 | tf_op jit(solution)/shard_map/ppermute | solution.py:208
  55.7 15.8 %all-to-all-start.1 = ((bf16[8,24,512]{2,1,0:T(8,128)(2,1)}), bf16[8,24,512]{2,1,0:T(8,128)(2,1)S(1)}, u32[]{:S(2)}, u32[]{:S(2)}) async-start(bf16[8,24,512]{2,1,0:T(8,128)(2,1)} %get-tuple-element.8), calls=%async_computation.1 | async-start | bytes 393216 | tf_op jit(solution)/shard_map/all_to_all | solution.py:209
  59.3 12.1 %collective-permute-start.4 = (bf16[4,4,2,16,512]{4,3,2,1,0:T(8,128)(2,1)S(1)}, bf16[4,4,2,16,512]{4,3,2,1,0:T(8,128)(2,1)S(1)}, u32[]{:S(2)}, u32[]{:S(2)}) collective-permute-start(bf16[4,4,2,16,512]{4,3,2,1,0:T(8,128)(2,1)S(1)} %bitcast.9), channel_id=1, source_target_pairs={{0,8},{8,0},{1,9},{9,1},{2,10},{10,2},{3,11},{11,3},{4,12},{12,4},... | collective-permute-start | bytes 1572872 | tf_op jit(solution)/shard_map/ppermute | solution.py:213
  65.0 3.2 %copy-start = (bf16[2,4096,512]{2,1,0:T(8,128)(2,1)}, bf16[2,4096,512]{2,1,0:T(8,128)(2,1)S(1)}, u32[]{:S(2)}) copy-start(bf16[2,4096,512]{2,1,0:T(8,128)(2,1)S(1)} %lag_table.1.table_ref) | copy-start | bytes 25165828
  71.4 3.4 %copy-start.1 = (bf16[2,4096,512]{2,1,0:T(8,128)(2,1)S(1)}, bf16[2,4096,512]{2,1,0:T(8,128)(2,1)}, u32[]{:S(2)}) copy-start(bf16[2,4096,512]{2,1,0:T(8,128)(2,1)} %copy-done) | copy-start | bytes 25165828

commit v3 on v2

v3 whole, which is shorter than its diff:
```python
import math

import jax
import jax.numpy as jnp
from jax import lax
from jax.experimental import pallas as pl
from jax.experimental.pallas import tpu as pltpu
from jax.sharding import Mesh, PartitionSpec as P

NSAMP = 32768
LAGS = 512
SMOOTH = 64
EPSILON = 1e-06
FREQS = 4096
SLICE = 512
CH = 6
ROWS = 12
SG = 4
SEGS = 2
LANES = 128
QUARTER = FREQS // 4
INDEX_AT = 2 + CH + SEGS * CH


def unit_circle(residue):
    quarter = NSAMP // 4
    quadrant = (residue + quarter // 2) >> 13
    rest = (residue - quadrant * quarter).astype(jnp.float32) * (2.0 * math.pi / NSAMP)
    sq = rest * rest
    sine = rest * (1.0 + sq * (-1.0 / 6 + sq * (1.0 / 120 + sq * (-1.0 / 5040))))
    cosine = 1.0 + sq * (-0.5 + sq * (1.0 / 24 + sq * (-1.0 / 720 + sq * (1.0 / 40320))))
    swap = (quadrant & 1) == 1
    first = jnp.where(swap, sine, cosine)
    second = jnp.where(swap, cosine, sine)
    first = jnp.where(((quadrant + 1) & 2) == 2, -first, first)
    second = jnp.where((quadrant & 2) == 2, -second, second)
    return first, second


NEAR = ("42601375", "35710264", "20643157", "02175346", "13420657", "02643175", "31576024", "20467153")


def whiten_kernel(info_ref, pieces_ref, chan_ref, src_ref, keep_ref):
    block, place = info_ref[0], info_ref[1]
    cells = jnp.concatenate([pieces_ref[i] for i in range(FREQS // SLICE)], axis=1).astype(jnp.float32)
    real, imag = cells[0:ROWS], cells[ROWS : 2 * ROWS]
    amplitude = jnp.sqrt(real * real + imag * imag)
    edge = jnp.zeros((ROWS, LANES), jnp.float32)
    padded = jnp.concatenate([edge, amplitude, edge], axis=1)
    width = FREQS + 2 * LANES
    run = padded
    for step in (1, 2, 4, 8, 16, 32, 64):
        run = run + pltpu.roll(run, width - step, 1)
    windowed = pltpu.roll(run, SMOOTH, 1) + pltpu.roll(padded, width - SMOOTH, 1)
    windowed = windowed[:, LANES : LANES + FREQS]

    row = lax.broadcasted_iota(jnp.int32, (ROWS, LANES), 0)
    offsets = jnp.zeros((ROWS, LANES), jnp.int32)
    alive = jnp.zeros((ROWS, LANES), jnp.int32)
    for k in range(SEGS):
        for c in range(CH):
            offsets = jnp.where(row == k * CH + c, info_ref[2 + CH + k * CH + c], offsets)
            alive = jnp.where(row == k * CH + c, info_ref[2 + c], alive)
    alive = alive.astype(jnp.float32)
    bins = lax.broadcasted_iota(jnp.int32, (ROWS, FREQS), 1)
    counts = jnp.minimum(bins + SMOOTH, FREQS - 1) - jnp.maximum(bins - SMOOTH, 0) + 1
    smoothed = windowed / counts.astype(jnp.float32) + EPSILON
    scale = jnp.concatenate([alive] * (FREQS // LANES), axis=1) / smoothed
    wide_offsets = jnp.concatenate([offsets] * (FREQS // LANES), axis=1)
    cosine, sine = unit_circle(((bins + 1) * wide_offsets) & (NSAMP - 1))
    white = [
        ((real * cosine - imag * sine) * scale).astype(jnp.bfloat16).astype(jnp.float32),
        ((real * sine + imag * cosine) * scale).astype(jnp.bfloat16).astype(jnp.float32),
    ]
    for q in range(2):
        for i in range(4):
            keep_ref[i, q, 0:ROWS] = white[q][:, i * QUARTER : (i + 1) * QUARTER]
    both = jnp.concatenate(white, axis=0) * (1.0 / math.sqrt(SEGS))
    for i in range(FREQS // SLICE):
        chan_ref[i] = both[:, i * SLICE : (i + 1) * SLICE]

    code = jnp.int32(0)
    for group, line in enumerate(NEAR):
        packed = sum((int(to) // 2) << (2 * n) for n, to in enumerate(line))
        code = jnp.where(block // 8 == group, packed, code)
    quarter = (code >> (2 * place)) & 3
    picked = []
    for q in range(2):
        for k in range(SEGS):
            for r in range(SG):
                at = info_ref[INDEX_AT + block * SG + r] - block * CH + k * CH
                picked.append(keep_ref[quarter, q, pl.ds(at, 1), :])
    src_ref[...] = jnp.concatenate(picked, axis=0).astype(jnp.bfloat16)


INNER = 64


def halves_sum(first, second, low):
    return jnp.where(low, first, second) + pltpu.roll(jnp.where(low, second, first), 4, 0)


HALF = LAGS // 2
PAIRS = 2 * CH * 16


def correlate_kernel(
    core_ref, mine_ref, other_ref, chan_ref, out_ref,
    inner_ref, outer_ref, even_cross, odd_cross, even_table, odd_table, cos_sum, sin_sum, last_sum, sum_ref
):
    low = lax.broadcasted_iota(jnp.int32, (8, LANES), 0) < 4
    lane = lax.broadcasted_iota(jnp.int32, (INNER, LAGS), 1)
    lags = jnp.where(lane < HALF, lane, lane - (HALF - 1))
    row = lax.broadcasted_iota(jnp.int32, (INNER, LAGS), 0)
    inner_ref[0], inner_ref[1] = unit_circle(((row + 1) * lags) & (NSAMP - 1))
    outer_ref[0], outer_ref[1] = unit_circle((row * INNER * lags) & (NSAMP - 1))

    def make_table(step, table_ref):
        for u in range(SLICE // INNER):
            at = step * (SLICE // INNER) + u
            ocos, osin = outer_ref[0, pl.ds(at, 1), :], outer_ref[1, pl.ds(at, 1), :]
            for block in range(LAGS // LANES):
                lanes = slice(block * LANES, (block + 1) * LANES)
                wcos = jnp.broadcast_to(ocos[:, lanes], (16, LANES))
                wsin = jnp.broadcast_to(osin[:, lanes], (16, LANES))
                for i in range(INNER // 16):
                    rows = slice(i * 16, i * 16 + 16)
                    icos, isin = inner_ref[0, rows, lanes], inner_ref[1, rows, lanes]
                    if block * LANES < HALF:
                        value = icos * wcos - isin * wsin
                    else:
                        value = isin * wcos + icos * wsin
                    put = u * INNER + i * 16
                    table_ref[put : put + 16, lanes] = value.astype(jnp.bfloat16)

    def cross(quarter, part, cross_ref):
        step = 2 * quarter + part
        for block in range(SLICE // LANES):
            lanes = slice(block * LANES, (block + 1) * LANES)
            from_lanes = slice(part * SLICE + block * LANES, part * SLICE + (block + 1) * LANES)
            chan = []
            for c in range(CH):
                tiles = []
                for q in range(2):
                    base = q * ROWS
                    one = chan_ref[step, base + c : base + c + 1, lanes]
                    two = chan_ref[step, base + CH + c : base + CH + c + 1, lanes]
                    tiles.append(
                        jnp.where(low, jnp.broadcast_to(one, (8, LANES)), jnp.broadcast_to(two, (8, LANES)))
                    )
                chan.append(tiles)
            for half, src_ref in enumerate((mine_ref, other_ref)):
                sources = [src_ref[quarter, x, :, from_lanes].astype(jnp.float32) for x in range(4)]
                for c in range(CH):
                    creal, cimag = chan[c]
                    reals, imags = [], []
                    for x in range(4):
                        sreal, simag = sources[x][0:8], sources[x][8:16]
                        reals.append(creal * sreal + cimag * simag)
                        imags.append(cimag * sreal - creal * simag)
                    at = half * CH * 16 + c * 16
                    for q, got in enumerate((reals, imags)):
                        rows = jnp.concatenate(
                            [halves_sum(got[0], got[1], low), halves_sum(got[2], got[3], low)], axis=0
                        ).astype(jnp.bfloat16)
                        cross_ref[q, at : at + 16, lanes] = rows
                        if q == 0:
                            last_sum[at : at + 16] += rows.astype(jnp.float32)

    def add(cross_ref, table_ref):
        cos_sum[...] += jnp.dot(cross_ref[0], table_ref[:, :HALF], preferred_element_type=jnp.float32)
        sin_sum[...] += jnp.dot(cross_ref[1], table_ref[:, HALF:], preferred_element_type=jnp.float32)

    cos_sum[...] = jnp.zeros_like(cos_sum)
    sin_sum[...] = jnp.zeros_like(sin_sum)
    last_sum[...] = jnp.zeros_like(last_sum)
    steps = FREQS // SLICE
    make_table(0, even_table)
    cross(0, 0, even_cross)

    def pair(i, carry):
        make_table(2 * i + 1, odd_table)
        cross(i, 1, odd_cross)
        add(even_cross, even_table)
        make_table(2 * i + 2, even_table)
        cross(i + 1, 0, even_cross)
        add(odd_cross, odd_table)
        return carry

    lax.fori_loop(0, steps // 2 - 1, pair, 0)
    make_table(steps - 1, odd_table)
    cross(steps // 2 - 1, 1, odd_cross)
    add(even_cross, even_table)
    add(odd_cross, odd_table)

    period = lax.broadcasted_iota(jnp.int32, (8, LANES), 1) + 1
    wave = unit_circle((period * HALF) & (NSAMP - 1))[0].astype(jnp.bfloat16).astype(jnp.float32)
    cos_last = jnp.sum(last_sum[...] * wave[0:1], axis=1, keepdims=True)
    cosines, sines = cos_sum[...], sin_sum[...]
    lane = lax.broadcasted_iota(jnp.int32, (PAIRS, HALF), 1)
    positive = cosines - jnp.where(lane == 0, 0.0, pltpu.roll(sines, 1, 1))
    negative = jnp.where(lane == HALF - 1, cos_last, pltpu.roll(cosines, HALF - 1, 1)) + sines
    first = negative.astype(jnp.bfloat16)
    rest = negative - first.astype(jnp.float32)
    second = rest.astype(jnp.bfloat16)
    third = (rest - second.astype(jnp.float32)).astype(jnp.bfloat16)
    mirror = (
        lax.broadcasted_iota(jnp.int32, (HALF, HALF), 0) + lax.broadcasted_iota(jnp.int32, (HALF, HALF), 1)
        == HALF - 1
    ).astype(jnp.float32).astype(jnp.bfloat16)
    flipped = [jnp.dot(t, mirror, preferred_element_type=jnp.float32) for t in (first, second, third)]
    factor = 1.0 / math.sqrt(FREQS)
    sum_ref[:, :, :, :HALF] = ((flipped[0] + flipped[1] + flipped[2]) * factor).reshape(2, CH, 16, HALF)
    sum_ref[:, :, :, HALF:] = (positive * factor).reshape(2, CH, 16, HALF)

    core = core_ref[0]
    for c in range(CH):
        zero, one = sum_ref[core, c], sum_ref[1 - core, c]
        for x in range(4):
            rows = slice(x * 4, x * 4 + 4)
            out_ref[c, x * 8 : x * 8 + 8, :] = jnp.concatenate([zero[rows], one[rows]], axis=0)


def scattered():
    pairs = []
    for group in range(8):
        for n in range(8):
            pairs.append((group * 8 + n, int(NEAR[group][n]) * 8 + group))
    return pairs


def body(spectra, dead_mask, seg_offsets, src_index):
    pos = {axis: lax.axis_index(axis).astype(jnp.int32) for axis in ("y", "h", "x", "c", "n")}
    wide_pos = ((pos["y"] * 2 + pos["h"]) * 4 + pos["x"]) * 2 + pos["c"]
    rows = jnp.transpose(spectra, (2, 1, 0, 3)).reshape(2 * ROWS, SLICE)
    info = jnp.concatenate(
        [jnp.stack([wide_pos, pos["n"]]), dead_mask, seg_offsets.T.reshape(SEGS * CH), src_index]
    )
    rows, info = lax.optimization_barrier((rows, info))
    pieces = lax.all_to_all(jnp.broadcast_to(rows[None], (8, 2 * ROWS, SLICE)), "n", 0, 0)

    vmem = pl.BlockSpec(memory_space=pltpu.VMEM)
    smem = pl.BlockSpec(memory_space=pltpu.SMEM)
    chan, src_out = pl.pallas_call(
        whiten_kernel,
        out_shape=(
            jax.ShapeDtypeStruct((FREQS // SLICE, 2 * ROWS, SLICE), jnp.float32),
            jax.ShapeDtypeStruct((16, QUARTER), jnp.bfloat16),
        ),
        in_specs=[smem, vmem],
        out_specs=(vmem, vmem),
        scratch_shapes=[pltpu.VMEM((4, 2, 16, QUARTER), jnp.float32)],
        compiler_params=pltpu.CompilerParams(vmem_limit_bytes=32 * 2**20),
        name="whiten",
    )(info, pieces)

    moved = lax.ppermute(src_out, ("y", "h", "n"), scattered())
    mine = lax.all_to_all(jnp.broadcast_to(moved[None], (16,) + moved.shape), ("y", "x"), 0, 0)
    mine = mine.reshape((4, 4) + moved.shape)
    other = lax.ppermute(mine, "c", [(0, 1), (1, 0)])

    out = pl.pallas_call(
        correlate_kernel,
        in_specs=[smem, vmem, vmem, vmem],
        out_specs=vmem,
        scratch_shapes=[
            pltpu.VMEM((2, INNER, LAGS), jnp.float32),
            pltpu.VMEM((2, FREQS // INNER, LAGS), jnp.float32),
            pltpu.VMEM((2, PAIRS, SLICE), jnp.bfloat16),
            pltpu.VMEM((2, PAIRS, SLICE), jnp.bfloat16),
            pltpu.VMEM((SLICE, LAGS), jnp.bfloat16),
            pltpu.VMEM((SLICE, LAGS), jnp.bfloat16),
            pltpu.VMEM((PAIRS, HALF), jnp.float32),
            pltpu.VMEM((PAIRS, HALF), jnp.float32),
            pltpu.VMEM((PAIRS, LANES), jnp.float32),
            pltpu.VMEM((2, CH, 16, LAGS), jnp.float32),
        ],
        out_shape=jax.ShapeDtypeStruct((CH, 32, LAGS), jnp.float32),
        compiler_params=pltpu.CompilerParams(vmem_limit_bytes=20 * 2**20),
        name="correlate",
    )(pos["c"].reshape(1), mine, other, chan)
    return jnp.transpose(out, (1, 0, 2))


def solution(mesh):
    parts = Mesh(mesh.devices.reshape(4, 2, 4, 2, 8), ("y", "h", "x", "c", "n"))
    wide = ("y", "h", "x", "c")
    placed = (P(wide, None, None, "n"), P(wide), P(wide, None), P())
    return jax.shard_map(
        body, mesh=parts, in_specs=placed, out_specs=P("n", wide, None), check_vma=False
    )
```

time: 82.3 us -> 68.6 us (0.83)
  the two profiles are of different devices: /device:TPU:2 before, /device:TPU:33 now
where the time goes in v3:
time: 68.6 us; the launch traced here: 68.3 us
  blocking collectives  37.5 us (55%)
  starting transfers between devices  14.7 us (21%)
  Pallas kernels  8.2 us (12%)
  waiting for transfers between devices  6.25 us (9%)
  local copies, waits for them, and re-layouts  1.61 us (2%)
    all_to_all x1, blocking collectives, body(): lax.all_to_all(jnp.broadcast_to(rows[None], (8, 2 * ROWS, SLICE)), 'n', 0...  21.1 us
    all_to_all x1, blocking collectives, body(): lax.all_to_all(jnp.broadcast_to(moved[None], (16,) + moved.shape), ('y',...  16.3 us
    ppermute x1, starting transfers between devices, body(): other = lax.ppermute(mine, 'c', [(0, 1), (1, 0)])  9.98 us
    pallas_call x1, Pallas kernels, body(): pl.pallas_call(correlate_kernel, in_specs=[smem, vmem, vmem, vmem], out_s...  6.39 us
    ppermute x1, starting transfers between devices, body(): moved = lax.ppermute(src_out, ('y', 'h', 'n'), scattered())  4.76 us
    ppermute x1, waiting for transfers between devices, body(): moved = lax.ppermute(src_out, ('y', 'h', 'n'), scattered())  4.74 us
    pallas_call x1, Pallas kernels, body(): pl.pallas_call(whiten_kernel, out_shape=(jax.ShapeDtypeStruct((FREQS // S...  1.81 us
    ppermute x1, waiting for transfers between devices, body(): other = lax.ppermute(mine, 'c', [(0, 1), (1, 0)])  1.51 us
  transfers between devices with their start and end apart: 2, of which 2 were waited for; matrix products, arithmetic and copies ran while one was open for 0% of the time, Pallas kernels for 0%

profile of v3, /device:TPU:33, one launch (start us, length us, event | category | flops | bytes accessed | tf_op | source)
XLA Modules:
  0.0 68.3 jit_solution(9481718354476119582)
XLA Ops:
  0.0 0.0 copy-start
  0.0 0.0 copy-start.3
  0.0 0.7 %copy-done.3 = s32[6,2]{0,1:T(2,128)S(1)} copy-done((s32[6,2]{0,1:T(2,128)S(1)}, s32[6,2]{0,1:T(2,128)}, u32[]{:S(2)}) %copy-start.3) | copy-done | bytes 72
  0.7 0.1 reshape.16
  0.8 0.0 copy-done
  0.8 0.0 copy-start.1
  0.8 0.0 copy-start.2
  0.8 0.7 copy-done.1
  1.5 0.0 copy-done.2
  1.5 0.1 concatenate.3.info_ref
  1.6 21.1 %all_to_all.10.pieces_ref = bf16[8,24,512]{2,1,0:T(8,128)(2,1)S(1)} all-to-all(bf16[8,24,512]{2,1,0:T(8,128)(2,1)S(1)} %broadcast_in_dim.4), channel_id=1, replica_groups=mesh['y'=4,'h'=2,'x'=4,'c'=2,'n'=8] {'n'}, dimensions={0} | all-to-all | bytes 393216 | tf_op jit(solution)/shard_map/all_to_all | solution.py:240
  22.7 1.8 %whiten.1 = (f32[8,24,512]{2,1,0:T(8,128)S(1)}, bf16[16,1024]{1,0:T(8,128)(2,1)S(1)}) custom-call(s32[276]{0:T(512)S(1)} %concatenate.3.info_ref, bf16[8,24,512]{2,1,0:T(8,128)(2,1)S(1)} %all_to_all.10.pieces_ref), custom_call_target="tpu_custom_call" | custom-call | tf_op jit(solution)/shard_map/whiten/pallas_call | solution.py:244
  24.6 4.8 %collective-permute-start = (bf16[16,1024]{1,0:T(8,128)(2,1)S(1)}, bf16[16,1024]{1,0:T(8,128)(2,1)S(1)}, u32[]{:S(2)}, u32[]{:S(2)}) collective-permute-start(bf16[16,1024]{1,0:T(8,128)(2,1)S(1)} %get-tuple-element.11), channel_id=1, source_target_pairs={{0,256},{1,128},{2,384},{3,0},{4,64},{5,192},{6,448},{7,320},{64,1... | collective-permute-start | bytes 98312 | tf_op jit(solution)/shard_map/ppermute | solution.py:257
  29.3 4.7 %collective-permute-done = bf16[16,1024]{1,0:T(8,128)(2,1)S(1)} collective-permute-done((bf16[16,1024]{1,0:T(8,128)(2,1)S(1)}, bf16[16,1024]{1,0:T(8,128)(2,1)S(1)}, u32[]{:S(2)}, u32[]{:S(2)}) %collective-permute-start) | collective-permute-done | bytes 32800 | tf_op jit(solution)/shard_map/ppermute | solution.py:257
  34.1 16.3 %all_to_all.11 = bf16[16,16,1024]{2,1,0:T(8,128)(2,1)S(1)} all-to-all(bf16[16,16,1024]{2,1,0:T(8,128)(2,1)S(1)} %broadcast_in_dim.5), channel_id=1, replica_groups=mesh['y'=4,'h'=2,'x'=4,'c'=2,'n'=8] {'y','x'}, dimensions={0} | all-to-all | bytes 1048576 | tf_op jit(solution)/shard_map/all_to_all | solution.py:258
  50.5 10.0 %collective-permute-start.1 = (bf16[4,4,16,1024]{3,2,1,0:T(8,128)(2,1)S(1)}, bf16[4,4,16,1024]{3,2,1,0:T(8,128)(2,1)S(1)}, u32[]{:S(2)}, u32[]{:S(2)}) collective-permute-start(bf16[4,4,16,1024]{3,2,1,0:T(8,128)(2,1)S(1)} %bitcast.7), channel_id=1, source_target_pairs={{0,8},{8,0},{1,9},{9,1},{2,10},{10,2},{3,11},{11,3},{4,12},{12,4},... | collective-permute-start | bytes 1572872 | tf_op jit(solution)/shard_map/ppermute | solution.py:260
  60.4 1.5 %collective-permute-done.1.other_ref = bf16[4,4,16,1024]{3,2,1,0:T(8,128)(2,1)S(1)} collective-permute-done((bf16[4,4,16,1024]{3,2,1,0:T(8,128)(2,1)S(1)}, bf16[4,4,16,1024]{3,2,1,0:T(8,128)(2,1)S(1)}, u32[]{:S(2)}, u32[]{:S(2)}) %collective-permute-start.1) | collective-permute-done | bytes 524320 | tf_op jit(solution)/shard_map/ppermute | solution.py:260
  62.0 6.4 %correlate.1 = f32[6,32,512]{2,1,0:T(8,128)} custom-call(s32[1]{0:T(128)} %bitcast.core_ref, bf16[4,4,16,1024]{3,2,1,0:T(8,128)(2,1)S(1)} %bitcast.8, bf16[4,4,16,1024]{3,2,1,0:T(8,128)(2,1)S(1)} %collective-permute-done.1.other_ref, f32[8,24,512]{2,1,0:T(8,128)S(1)} %get-tuple-element.12.chan_ref), custom_call_target="tpu_custom_call" | custom-call | tf_op jit(solution)/shard_map/correlate/pallas_call | solution.py:262
  (4 shorter events, 0.1 us)
Async XLA Ops:
  0.0 0.8 %copy-start = (bf16[6,2,2,512]{3,2,1,0:T(2,128)(2,1)S(1)}, bf16[6,2,2,512]{3,2,1,0:T(2,128)(2,1)}, u32[]{:S(2)}) copy-start(bf16[6,2,2,512]{3,2,1,0:T(2,128)(2,1)} %param.4) | copy-start | bytes 73732
  0.0 0.7 %copy-start.3 = (s32[6,2]{0,1:T(2,128)S(1)}, s32[6,2]{0,1:T(2,128)}, u32[]{:S(2)}) copy-start(s32[6,2]{0,1:T(2,128)} %param.6) | copy-start | bytes 148
  0.8 0.7 copy-start.1
  0.8 0.7 copy-start.2
  24.6 9.5 %collective-permute-start = (bf16[16,1024]{1,0:T(8,128)(2,1)S(1)}, bf16[16,1024]{1,0:T(8,128)(2,1)S(1)}, u32[]{:S(2)}, u32[]{:S(2)}) collective-permute-start(bf16[16,1024]{1,0:T(8,128)(2,1)S(1)} %get-tuple-element.11), channel_id=1, source_target_pairs={{0,256},{1,128},{2,384},{3,0},{4,64},{5,192},{6,448},{7,320},{64,1... | collective-permute-start | bytes 98312 | tf_op jit(solution)/shard_map/ppermute | solution.py:257
  50.5 11.5 %collective-permute-start.1 = (bf16[4,4,16,1024]{3,2,1,0:T(8,128)(2,1)S(1)}, bf16[4,4,16,1024]{3,2,1,0:T(8,128)(2,1)S(1)}, u32[]{:S(2)}, u32[]{:S(2)}) collective-permute-start(bf16[4,4,16,1024]{3,2,1,0:T(8,128)(2,1)S(1)} %bitcast.7), channel_id=1, source_target_pairs={{0,8},{8,0},{1,9},{9,1},{2,10},{10,2},{3,11},{11,3},{4,12},{12,4},... | collective-permute-start | bytes 1572872 | tf_op jit(solution)/shard_map/ppermute | solution.py:260

commit v4 on v3

v4 whole, which is shorter than its diff:
```python
import math

import jax
import jax.numpy as jnp
from jax import lax
from jax.experimental import pallas as pl
from jax.experimental.pallas import tpu as pltpu
from jax.sharding import Mesh, PartitionSpec as P

NSAMP = 32768
LAGS = 512
SMOOTH = 64
EPSILON = 1e-06
FREQS = 4096
SLICE = 512
CH = 6
ROWS = 12
SG = 4
SEGS = 2
LANES = 128
QUARTER = FREQS // 4


def unit_circle(residue):
    quarter = NSAMP // 4
    quadrant = (residue + quarter // 2) >> 13
    rest = (residue - quadrant * quarter).astype(jnp.float32) * (2.0 * math.pi / NSAMP)
    sq = rest * rest
    sine = rest * (1.0 + sq * (-1.0 / 6 + sq * (1.0 / 120 + sq * (-1.0 / 5040))))
    cosine = 1.0 + sq * (-0.5 + sq * (1.0 / 24 + sq * (-1.0 / 720 + sq * (1.0 / 40320))))
    swap = (quadrant & 1) == 1
    first = jnp.where(swap, sine, cosine)
    second = jnp.where(swap, cosine, sine)
    first = jnp.where(((quadrant + 1) & 2) == 2, -first, first)
    second = jnp.where((quadrant & 2) == 2, -second, second)
    return first, second


def turned(pair, by):
    return pair[0] * by[0] - pair[1] * by[1], pair[1] * by[0] + pair[0] * by[1]


NEAR = ("42601375", "35710264", "20643157", "02175346", "13420657", "02643175", "31576024", "20467153")


def whiten_kernel(info_ref, pieces_ref, chan_ref, src_ref, keep_ref):
    block, place = info_ref[4, 0], info_ref[4, 1]
    cells = jnp.concatenate([pieces_ref[i] for i in range(FREQS // SLICE)], axis=1).astype(jnp.float32)
    real, imag = cells[0:ROWS], cells[ROWS : 2 * ROWS]
    amplitude = jnp.sqrt(real * real + imag * imag)
    edge = jnp.zeros((ROWS, LANES), jnp.float32)
    padded = jnp.concatenate([edge, amplitude, edge], axis=1)
    width = FREQS + 2 * LANES
    run = padded
    for step in (1, 2, 4, 8, 16, 32, 64):
        run = run + pltpu.roll(run, width - step, 1)
    windowed = pltpu.roll(run, SMOOTH, 1) + pltpu.roll(padded, width - SMOOTH, 1)
    windowed = windowed[:, LANES : LANES + FREQS]

    row = lax.broadcasted_iota(jnp.int32, (ROWS, LANES), 0)
    offsets = jnp.zeros((ROWS, LANES), jnp.int32)
    alive = jnp.zeros((ROWS, LANES), jnp.int32)
    for k in range(SEGS):
        for c in range(CH):
            offsets = jnp.where(row == k * CH + c, info_ref[1 + k, c], offsets)
            alive = jnp.where(row == k * CH + c, info_ref[3, c], alive)
    alive = alive.astype(jnp.float32)
    lane = lax.broadcasted_iota(jnp.int32, (ROWS, LANES), 1)
    head = windowed[:, :LANES] / (jnp.minimum(lane, SMOOTH) + (SMOOTH + 1)).astype(jnp.float32)
    tail = windowed[:, FREQS - LANES :] / (
        jnp.minimum(LANES - 1 - lane, SMOOTH) + (SMOOTH + 1)
    ).astype(jnp.float32)
    middle = windowed[:, LANES : FREQS - LANES] * (1.0 / (2 * SMOOTH + 1))
    smoothed = jnp.concatenate([head, middle, tail], axis=1) + EPSILON
    scale = jnp.concatenate([alive] * (FREQS // LANES), axis=1) / smoothed

    inner = unit_circle(((lane + 1) * offsets) & (NSAMP - 1))
    groups = [inner]
    for j in (1, 2, 3):
        groups.append(turned(inner, unit_circle((j * LANES * offsets) & (NSAMP - 1))))
    angles = list(groups)
    for j in range(1, FREQS // (4 * LANES)):
        outer = unit_circle((j * 4 * LANES * offsets) & (NSAMP - 1))
        angles += [turned(group, outer) for group in groups]
    cosine = jnp.concatenate([pair[0] for pair in angles], axis=1)
    sine = jnp.concatenate([pair[1] for pair in angles], axis=1)
    white = [
        ((real * cosine - imag * sine) * scale).astype(jnp.bfloat16).astype(jnp.float32),
        ((real * sine + imag * cosine) * scale).astype(jnp.bfloat16).astype(jnp.float32),
    ]
    for q in range(2):
        for i in range(4):
            keep_ref[i, q, 0:ROWS] = white[q][:, i * QUARTER : (i + 1) * QUARTER]
        scaled = white[q] * (1.0 / math.sqrt(SEGS))
        for i in range(FREQS // SLICE):
            chan_ref[i, q] = scaled[:, i * SLICE : (i + 1) * SLICE]

    code = jnp.int32(0)
    for group, line in enumerate(NEAR):
        packed = sum((int(to) // 2) << (2 * n) for n, to in enumerate(line))
        code = jnp.where(block // 8 == group, packed, code)
    quarter = (code >> (2 * place)) & 3
    picked = []
    for q in range(2):
        for k in range(SEGS):
            for r in range(SG):
                at = info_ref[0, block * SG + r] - block * CH + k * CH
                picked.append(keep_ref[quarter, q, pl.ds(at, 1), :])
    src_ref[...] = jnp.concatenate(picked, axis=0).astype(jnp.bfloat16)


INNER = 64


HALF = LAGS // 2
PAIRS = 2 * CH * 16


def table_kernel(after_ref, table_ref, inner_ref, outer_ref):
    lane = lax.broadcasted_iota(jnp.int32, (INNER, LAGS), 1)
    lags = jnp.where(lane < HALF, lane, lane - (HALF - 1))
    row = lax.broadcasted_iota(jnp.int32, (INNER, LAGS), 0)
    inner_ref[0], inner_ref[1] = unit_circle(((row + 1) * lags) & (NSAMP - 1))
    for q, values in enumerate(unit_circle((row * INNER * lags) & (NSAMP - 1))):
        for block in range(LAGS // LANES):
            outer_ref[q, block] = values[:, block * LANES : (block + 1) * LANES]
    for block in range(LAGS // LANES):
        lanes = slice(block * LANES, (block + 1) * LANES)
        for i in range(INNER // 16):
            rows = slice(i * 16, i * 16 + 16)
            icos, isin = inner_ref[0, rows, lanes], inner_ref[1, rows, lanes]

            def put(at, carry, icos=icos, isin=isin, block=block, lanes=lanes, i=i):
                wcos = jnp.broadcast_to(outer_ref[0, block, pl.ds(at, 1), :], (16, LANES))
                wsin = jnp.broadcast_to(outer_ref[1, block, pl.ds(at, 1), :], (16, LANES))
                if lanes.start < HALF:
                    value = icos * wcos - isin * wsin
                else:
                    value = isin * wcos + icos * wsin
                table_ref[at, i * 16 : i * 16 + 16, lanes] = value.astype(jnp.bfloat16)
                return carry

            lax.fori_loop(0, FREQS // INNER, put, 0, unroll=16)


def correlate_kernel(
    core_ref, mine_ref, other_ref, chan_ref, table_ref, out_ref,
    even_cross, odd_cross, cos_sum, sin_sum, last_sum, sum_ref
):
    low = lax.broadcasted_iota(jnp.int32, (8, LANES), 0) < 4

    def cross(quarter, part, cross_ref):
        step = 2 * quarter + part
        for block in range(SLICE // LANES):
            lanes = slice(block * LANES, (block + 1) * LANES)
            from_lanes = slice(part * SLICE + block * LANES, part * SLICE + (block + 1) * LANES)
            for half, src_ref in enumerate((mine_ref, other_ref)):
                tiles = []
                for x in (0, 2):
                    first = src_ref[quarter, x, :, from_lanes].astype(jnp.float32)
                    second = src_ref[quarter, x + 1, :, from_lanes].astype(jnp.float32)
                    parts = []
                    for q in range(2):
                        one, two = first[q * 8 : q * 8 + 8], second[q * 8 : q * 8 + 8]
                        parts.append(jnp.where(low, one, pltpu.roll(two, 4, 0)))
                        parts.append(jnp.where(low, pltpu.roll(one, 4, 0), two))
                    tiles.append(parts)
                for c in range(CH):
                    creal, cimag = [
                        [
                            jnp.broadcast_to(
                                chan_ref[step, q, k * CH + c : k * CH + c + 1, lanes],
                                (8, LANES),
                            )
                            for k in range(SEGS)
                        ]
                        for q in range(2)
                    ]
                    reals, imags = [], []
                    for real0, real1, imag0, imag1 in tiles:
                        reals.append(
                            (creal[0] * real0 + cimag[0] * imag0) + (creal[1] * real1 + cimag[1] * imag1)
                        )
                        imags.append(
                            (cimag[0] * real0 - creal[0] * imag0) + (cimag[1] * real1 - creal[1] * imag1)
                        )
                    at = half * CH * 16 + c * 16
                    for q, got in enumerate((reals, imags)):
                        rows = jnp.concatenate(got, axis=0).astype(jnp.bfloat16)
                        cross_ref[q, at : at + 16, lanes] = rows
                        if q == 0:
                            last_sum[at : at + 16] += rows.astype(jnp.float32)

    def add(step, cross_ref):
        chunk = table_ref[pl.ds(step * (SLICE // INNER), SLICE // INNER)].reshape(SLICE, LAGS)
        cos_sum[...] += jnp.dot(cross_ref[0], chunk[:, :HALF], preferred_element_type=jnp.float32)
        sin_sum[...] += jnp.dot(cross_ref[1], chunk[:, HALF:], preferred_element_type=jnp.float32)

    cos_sum[...] = jnp.zeros_like(cos_sum)
    sin_sum[...] = jnp.zeros_like(sin_sum)
    last_sum[...] = jnp.zeros_like(last_sum)
    steps = FREQS // SLICE
    cross(0, 0, even_cross)

    def pair(i, carry):
        cross(i, 1, odd_cross)
        add(2 * i, even_cross)
        cross(i + 1, 0, even_cross)
        add(2 * i + 1, odd_cross)
        return carry

    lax.fori_loop(0, steps // 2 - 1, pair, 0)
    cross(steps // 2 - 1, 1, odd_cross)
    add(steps - 2, even_cross)
    add(steps - 1, odd_cross)

    period = lax.broadcasted_iota(jnp.int32, (8, LANES), 1) + 1
    wave = unit_circle((period * HALF) & (NSAMP - 1))[0].astype(jnp.bfloat16).astype(jnp.float32)
    cos_last = jnp.sum(last_sum[...] * wave[0:1], axis=1, keepdims=True)
    cosines, sines = cos_sum[...], sin_sum[...]
    lane = lax.broadcasted_iota(jnp.int32, (PAIRS, HALF), 1)
    positive = cosines - jnp.where(lane == 0, 0.0, pltpu.roll(sines, 1, 1))
    negative = jnp.where(lane == HALF - 1, cos_last, pltpu.roll(cosines, HALF - 1, 1)) + sines
    first = negative.astype(jnp.bfloat16)
    rest = negative - first.astype(jnp.float32)
    second = rest.astype(jnp.bfloat16)
    third = (rest - second.astype(jnp.float32)).astype(jnp.bfloat16)
    mirror = (
        lax.broadcasted_iota(jnp.int32, (HALF, HALF), 0) + lax.broadcasted_iota(jnp.int32, (HALF, HALF), 1)
        == HALF - 1
    ).astype(jnp.float32).astype(jnp.bfloat16)
    flipped = [jnp.dot(t, mirror, preferred_element_type=jnp.float32) for t in (first, second, third)]
    factor = 1.0 / math.sqrt(FREQS)
    sum_ref[:, :, :, :HALF] = ((flipped[0] + flipped[1] + flipped[2]) * factor).reshape(2, CH, 16, HALF)
    sum_ref[:, :, :, HALF:] = (positive * factor).reshape(2, CH, 16, HALF)

    core = core_ref[0]
    for c in range(CH):
        zero, one = sum_ref[core, c], sum_ref[1 - core, c]
        for x in range(4):
            rows = slice(x * 4, x * 4 + 4)
            out_ref[c, x * 8 : x * 8 + 8, :] = jnp.concatenate([zero[rows], one[rows]], axis=0)


def scattered():
    pairs = []
    for group in range(8):
        for n in range(8):
            pairs.append((group * 8 + n, int(NEAR[group][n]) * 8 + group))
    return pairs


def body(spectra, dead_mask, seg_offsets, src_index):
    pos = {axis: lax.axis_index(axis).astype(jnp.int32) for axis in ("y", "h", "x", "c", "n")}
    wide_pos = ((pos["y"] * 2 + pos["h"]) * 4 + pos["x"]) * 2 + pos["c"]
    rows = jnp.transpose(spectra, (2, 1, 0, 3)).reshape(2 * ROWS, SLICE)
    width = src_index.shape[0]
    info = jnp.concatenate(
        [
            src_index[None],
            jnp.pad(seg_offsets.T, ((0, 0), (0, width - CH))),
            jnp.pad(dead_mask, (0, width - CH))[None],
            jnp.pad(jnp.stack([wide_pos, pos["n"]]), (0, width - 2))[None],
        ]
    )
    pieces = lax.all_to_all(jnp.broadcast_to(rows[None], (8, 2 * ROWS, SLICE)), "n", 0, 0)

    vmem = pl.BlockSpec(memory_space=pltpu.VMEM)
    smem = pl.BlockSpec(memory_space=pltpu.SMEM)
    chan, src_out = pl.pallas_call(
        whiten_kernel,
        out_shape=(
            jax.ShapeDtypeStruct((FREQS // SLICE, 2, ROWS, SLICE), jnp.float32),
            jax.ShapeDtypeStruct((16, QUARTER), jnp.bfloat16),
        ),
        in_specs=[smem, vmem],
        out_specs=(vmem, vmem),
        scratch_shapes=[pltpu.VMEM((4, 2, 16, QUARTER), jnp.float32)],
        compiler_params=pltpu.CompilerParams(vmem_limit_bytes=32 * 2**20),
        name="whiten",
    )(info, pieces)

    moved = lax.ppermute(src_out, ("y", "h", "n"), scattered())
    mine = lax.all_to_all(jnp.broadcast_to(moved[None], (16,) + moved.shape), ("y", "x"), 0, 0)
    mine = mine.reshape((4, 4) + moved.shape)
    other = lax.ppermute(mine, "c", [(0, 1), (1, 0)])

    table = pl.pallas_call(
        table_kernel,
        in_specs=[pl.BlockSpec(memory_space=pl.ANY)],
        out_specs=vmem,
        scratch_shapes=[
            pltpu.VMEM((2, INNER, LAGS), jnp.float32),
            pltpu.VMEM((2, LAGS // LANES, FREQS // INNER, LANES), jnp.float32),
        ],
        out_shape=jax.ShapeDtypeStruct((FREQS // INNER, INNER, LAGS), jnp.bfloat16),
        compiler_params=pltpu.CompilerParams(vmem_limit_bytes=16 * 2**20),
        cost_estimate=pl.CostEstimate(flops=4 * FREQS * LAGS, bytes_accessed=2 * FREQS * LAGS, transcendentals=0),
        name="lag_table",
    )(mine)

    out = pl.pallas_call(
        correlate_kernel,
        in_specs=[smem, vmem, vmem, vmem, vmem],
        out_specs=vmem,
        scratch_shapes=[
            pltpu.VMEM((2, PAIRS, SLICE), jnp.bfloat16),
            pltpu.VMEM((2, PAIRS, SLICE), jnp.bfloat16),
            pltpu.VMEM((PAIRS, HALF), jnp.float32),
            pltpu.VMEM((PAIRS, HALF), jnp.float32),
            pltpu.VMEM((PAIRS, LANES), jnp.float32),
            pltpu.VMEM((2, CH, 16, LAGS), jnp.float32),
        ],
        out_shape=jax.ShapeDtypeStruct((CH, 32, LAGS), jnp.float32),
        compiler_params=pltpu.CompilerParams(vmem_limit_bytes=20 * 2**20),
        name="correlate",
    )(pos["c"].reshape(1), mine, other, chan, table)
    return jnp.transpose(out, (1, 0, 2))


def solution(mesh):
    parts = Mesh(mesh.devices.reshape(4, 2, 4, 2, 8), ("y", "h", "x", "c", "n"))
    wide = ("y", "h", "x", "c")
    placed = (P(wide, None, None, "n"), P(wide), P(wide, None), P())
    return jax.shard_map(
        body, mesh=parts, in_specs=placed, out_specs=P("n", wide, None), check_vma=False
    )
```

time: 68.6 us -> 66.7 us (0.972)
  blocking collectives: 37.5 us -> 16.3 us
  starting transfers between devices: 14.7 us -> 26.8 us
  waiting for transfers between devices: 6.25 us -> 12.6 us
  other arithmetic: 0 us -> 0.78 us
    all_to_all x1 -> x0, blocking collectives: 21.1 us -> none  [body(): lax.all_to_all(jnp.broadcast_to(rows[None], (8, 2 * ROWS, SLICE)), 'n', 0...]
    all_to_all x0 -> x1, starting transfers between devices: none -> 12.1 us  [body(): lax.all_to_all(jnp.broadcast_to(rows[None], (8, 2 * ROWS, SLICE)), 'n', 0...]
    all_to_all x0 -> x1, waiting for transfers between devices: none -> 7.82 us  [body(): lax.all_to_all(jnp.broadcast_to(rows[None], (8, 2 * ROWS, SLICE)), 'n', 0...]
    ppermute x1, waiting for transfers between devices: 1.51 us -> 0.01 us  [body(): other = lax.ppermute(mine, 'c', [(0, 1), (1, 0)])]
    unnamed x8 -> x0, local copies, waits for them, and re-layouts: 1.36 us -> none
    transpose x1, local copies, waits for them, and re-layouts: 0.01 us -> 0.75 us  [body(): rows = jnp.transpose(spectra, (2, 1, 0, 3)).reshape(2 * ROWS, SLICE)]
    concatenate x0 -> x1, other arithmetic: none -> 0.71 us  [body(): jnp.concatenate([src_index[None], jnp.pad(seg_offsets.T, ((0, 0), (0, wid...]
    broadcast_in_dim x1 -> x2, local copies, waits for them, and re-layouts: 0.02 us -> 0.71 us  [body(): jnp.broadcast_to(rows[None], (8, 2 * ROWS, SLICE))]
  transfers between devices with their start and end apart: 2 -> 3, of which waited for: 2 -> 2; matrix products, arithmetic and copies ran while one was open for 0% -> 2% of each run, Pallas kernels for 0% -> 3%
where the time goes in v4:
time: 66.7 us; the launch traced here: 66.4 us
  starting transfers between devices  26.8 us (40%)
  blocking collectives  16.3 us (24%)
  waiting for transfers between devices  12.6 us (19%)
  Pallas kernels  7.67 us (11%)
  local copies, waits for them, and re-layouts  2.17 us (3%)
  other arithmetic  0.78 us (1%)
    all_to_all x1, blocking collectives, body(): lax.all_to_all(jnp.broadcast_to(moved[None], (16,) + moved.shape), ('y',...  16.3 us
    all_to_all x1, starting transfers between devices, body(): lax.all_to_all(jnp.broadcast_to(rows[None], (8, 2 * ROWS, SLICE)), 'n', 0...  12.1 us
    ppermute x1, starting transfers between devices, body(): other = lax.ppermute(mine, 'c', [(0, 1), (1, 0)])  9.98 us
    all_to_all x1, waiting for transfers between devices, body(): lax.all_to_all(jnp.broadcast_to(rows[None], (8, 2 * ROWS, SLICE)), 'n', 0...  7.82 us
    ppermute x1, starting transfers between devices, body(): moved = lax.ppermute(src_out, ('y', 'h', 'n'), scattered())  4.76 us
    ppermute x1, waiting for transfers between devices, body(): moved = lax.ppermute(src_out, ('y', 'h', 'n'), scattered())  4.74 us
    pallas_call x1, Pallas kernels, body(): pl.pallas_call(correlate_kernel, in_specs=[smem, vmem, vmem, vmem, vmem],...  4.14 us
    pallas_call x1, Pallas kernels, body(): pl.pallas_call(table_kernel, in_specs=[pl.BlockSpec(memory_space=pl.ANY)]...  1.8 us
  transfers between devices with their start and end apart: 3, of which 2 were waited for; matrix products, arithmetic and copies ran while one was open for 2% of the time, Pallas kernels for 3%

profile of v4, /device:TPU:33, one launch (start us, length us, event | category | flops | bytes accessed | tf_op | source)
XLA Modules:
  0.0 66.4 jit_solution(14136633241799931210)
XLA Ops:
  0.0 0.7 %copy.5 = bf16[2,2,6,512]{3,2,1,0:T(8,128)(2,1)S(1)} copy(bf16[2,2,6,512]{3,0,1,2:T(2,128)(2,1)} %bitcast.13) | data formatting | bytes 49152 | tf_op jit(solution)/shard_map/transpose | solution.py:256
  0.8 0.7 %broadcast_in_dim.26 = bf16[8,24,512]{2,1,0:T(8,128)(2,1)} broadcast(bf16[24,512]{1,0:T(8,128)(2,1)S(1)} %broadcast_in_dim.25), dimensions={1,2} | broadcast | bytes 221184 | tf_op jit(solution)/shard_map/broadcast_in_dim | solution.py:266
  1.5 12.1 %all-to-all-start = ((bf16[8,24,512]{2,1,0:T(8,128)(2,1)}), bf16[8,24,512]{2,1,0:T(8,128)(2,1)S(1)}, u32[]{:S(2)}, u32[]{:S(2)}) async-start(bf16[8,24,512]{2,1,0:T(8,128)(2,1)} %broadcast_in_dim.26), calls=%async_computation | async-start | bytes 393216 | tf_op jit(solution)/shard_map/all_to_all | solution.py:266
  13.5 0.1 pad_add_fusion.1
  13.6 0.7 pad.13
  14.3 0.7 %fusion.1.info_ref = s32[5,256]{1,0:T(8,128)S(1)} fusion(s32[2,6]{1,0:T(2,128)} %bitcast.16, s32[1,256]{1,0:T(1,128)S(1)} %bitcast.14, s32[1,256]{1,0:T(1,128)S(1)} %bitcast.15, s32[1,256]{1,0:T(1,128)} %bitcast.17), kind=kLoop, calls=%fused_computation.2 | loop fusion | flops 3840 | bytes 8240 | tf_op jit(solution)/shard_map/concatenate | solution.py:258
  15.0 7.8 %all-to-all-done.pieces_ref = bf16[8,24,512]{2,1,0:T(8,128)(2,1)S(1)} async-done(((bf16[8,24,512]{2,1,0:T(8,128)(2,1)}), bf16[8,24,512]{2,1,0:T(8,128)(2,1)S(1)}, u32[]{:S(2)}, u32[]{:S(2)}) %all-to-all-start) | async-done | bytes 196640 | tf_op jit(solution)/shard_map/all_to_all | solution.py:266
  22.8 1.7 %whiten.1 = (f32[8,2,12,512]{3,2,1,0:T(8,128)S(1)}, bf16[16,1024]{1,0:T(8,128)(2,1)S(1)}) custom-call(s32[5,256]{1,0:T(8,128)S(1)} %fusion.1.info_ref, bf16[8,24,512]{2,1,0:T(8,128)(2,1)S(1)} %all-to-all-done.pieces_ref), custom_call_target="tpu_custom_call" | custom-call | tf_op jit(solution)/shard_map/whiten/pallas_call | solution.py:270
  24.5 4.8 %collective-permute-start = (bf16[16,1024]{1,0:T(8,128)(2,1)S(1)}, bf16[16,1024]{1,0:T(8,128)(2,1)S(1)}, u32[]{:S(2)}, u32[]{:S(2)}) collective-permute-start(bf16[16,1024]{1,0:T(8,128)(2,1)S(1)} %get-tuple-element.7), channel_id=1, source_target_pairs={{0,256},{1,128},{2,384},{3,0},{4,64},{5,192},{6,448},{7,320},{64,1... | collective-permute-start | bytes 98312 | tf_op jit(solution)/shard_map/ppermute | solution.py:283
  29.3 4.7 %collective-permute-done = bf16[16,1024]{1,0:T(8,128)(2,1)S(1)} collective-permute-done((bf16[16,1024]{1,0:T(8,128)(2,1)S(1)}, bf16[16,1024]{1,0:T(8,128)(2,1)S(1)}, u32[]{:S(2)}, u32[]{:S(2)}) %collective-permute-start) | collective-permute-done | bytes 32800 | tf_op jit(solution)/shard_map/ppermute | solution.py:283
  34.1 16.3 %all_to_all.10 = bf16[16,16,1024]{2,1,0:T(8,128)(2,1)S(1)} all-to-all(bf16[16,16,1024]{2,1,0:T(8,128)(2,1)S(1)} %broadcast_in_dim.27), channel_id=1, replica_groups=mesh['y'=4,'h'=2,'x'=4,'c'=2,'n'=8] {'y','x'}, dimensions={0} | all-to-all | bytes 1048576 | tf_op jit(solution)/shard_map/all_to_all | solution.py:284
  50.4 10.0 %collective-permute-start.1 = (bf16[4,4,16,1024]{3,2,1,0:T(8,128)(2,1)S(1)}, bf16[4,4,16,1024]{3,2,1,0:T(8,128)(2,1)S(1)}, u32[]{:S(2)}, u32[]{:S(2)}) collective-permute-start(bf16[4,4,16,1024]{3,2,1,0:T(8,128)(2,1)S(1)} %bitcast.10), channel_id=1, source_target_pairs={{0,8},{8,0},{1,9},{9,1},{2,10},{10,2},{3,11},{11,3},{4,12},{12,4},... | collective-permute-start | bytes 1572872 | tf_op jit(solution)/shard_map/ppermute | solution.py:286
  60.4 1.8 %lag_table.1.table_ref = bf16[64,64,512]{2,1,0:T(8,128)(2,1)S(1)} custom-call(bf16[4,4,16,1024]{3,2,1,0:T(8,128)(2,1)S(1)} %bitcast.11), custom_call_target="tpu_custom_call" | custom-call | flops 8388608 | bytes 4194304 | tf_op jit(solution)/shard_map/lag_table/pallas_call | solution.py:288
  62.2 0.0 collective-permute-done.1.other_ref
  62.2 4.1 %correlate.1 = f32[6,32,512]{2,1,0:T(8,128)} custom-call(s32[1]{0:T(128)} %bitcast.core_ref, bf16[4,4,16,1024]{3,2,1,0:T(8,128)(2,1)S(1)} %bitcast.12, bf16[4,4,16,1024]{3,2,1,0:T(8,128)(2,1)S(1)} %collective-permute-done.1.other_ref, f32[8,2,12,512]{3,2,1,0:T(8,128)S(1)} %get-tuple-element.8.chan_ref, bf16[64,64,512]{2,1,0:T(8,128)(2,1)S(1)} %lag_table.1.table_ref), custom_call_target="tpu_custom_call" | custom-call | tf_op jit(solution)/shard_map/correlate/pallas_call | solution.py:302
  (3 shorter events, 0.1 us)
Async XLA Ops:
  1.5 21.3 %all-to-all-start = ((bf16[8,24,512]{2,1,0:T(8,128)(2,1)}), bf16[8,24,512]{2,1,0:T(8,128)(2,1)S(1)}, u32[]{:S(2)}, u32[]{:S(2)}) async-start(bf16[8,24,512]{2,1,0:T(8,128)(2,1)} %broadcast_in_dim.26), calls=%async_computation | async-start | bytes 393216 | tf_op jit(solution)/shard_map/all_to_all | solution.py:266
  24.5 9.5 %collective-permute-start = (bf16[16,1024]{1,0:T(8,128)(2,1)S(1)}, bf16[16,1024]{1,0:T(8,128)(2,1)S(1)}, u32[]{:S(2)}, u32[]{:S(2)}) collective-permute-start(bf16[16,1024]{1,0:T(8,128)(2,1)S(1)} %get-tuple-element.7), channel_id=1, source_target_pairs={{0,256},{1,128},{2,384},{3,0},{4,64},{5,192},{6,448},{7,320},{64,1... | collective-permute-start | bytes 98312 | tf_op jit(solution)/shard_map/ppermute | solution.py:283
  50.4 11.8 %collective-permute-start.1 = (bf16[4,4,16,1024]{3,2,1,0:T(8,128)(2,1)S(1)}, bf16[4,4,16,1024]{3,2,1,0:T(8,128)(2,1)S(1)}, u32[]{:S(2)}, u32[]{:S(2)}) collective-permute-start(bf16[4,4,16,1024]{3,2,1,0:T(8,128)(2,1)S(1)} %bitcast.10), channel_id=1, source_target_pairs={{0,8},{8,0},{1,9},{9,1},{2,10},{10,2},{3,11},{11,3},{4,12},{12,4},... | collective-permute-start | bytes 1572872 | tf_op jit(solution)/shard_map/ppermute | solution.py:286

commit v5 on v4

--- a/solution.py
+++ b/solution.py
@@ -18,7 +18,7 @@
 SG = 4
 SEGS = 2
 LANES = 128
-QUARTER = FREQS // 4
+SHARE = FREQS // 2
 
 
 def unit_circle(residue):
@@ -89,23 +89,23 @@
         ((real * sine + imag * cosine) * scale).astype(jnp.bfloat16).astype(jnp.float32),
     ]
     for q in range(2):
-        for i in range(4):
-            keep_ref[i, q, 0:ROWS] = white[q][:, i * QUARTER : (i + 1) * QUARTER]
+        for i in range(2):
+            keep_ref[i, q, 0:ROWS] = white[q][:, i * SHARE : (i + 1) * SHARE]
         scaled = white[q] * (1.0 / math.sqrt(SEGS))
         for i in range(FREQS // SLICE):
             chan_ref[i, q] = scaled[:, i * SLICE : (i + 1) * SLICE]
 
     code = jnp.int32(0)
     for group, line in enumerate(NEAR):
-        packed = sum((int(to) // 2) << (2 * n) for n, to in enumerate(line))
+        packed = sum((int(to) // 2 % 2) << n for n, to in enumerate(line))
         code = jnp.where(block // 8 == group, packed, code)
-    quarter = (code >> (2 * place)) & 3
+    upper = (code >> place) & 1
     picked = []
     for q in range(2):
         for k in range(SEGS):
             for r in range(SG):
                 at = info_ref[0, block * SG + r] - block * CH + k * CH
-                picked.append(keep_ref[quarter, q, pl.ds(at, 1), :])
+                picked.append(keep_ref[upper, q, pl.ds(at, 1), :])
     src_ref[...] = jnp.concatenate(picked, axis=0).astype(jnp.bfloat16)
 
 
@@ -149,16 +149,16 @@
 ):
     low = lax.broadcasted_iota(jnp.int32, (8, LANES), 0) < 4
 
-    def cross(quarter, part, cross_ref):
-        step = 2 * quarter + part
+    def cross(step, cross_ref):
+        upper, part = divmod(step, SHARE // SLICE)
         for block in range(SLICE // LANES):
             lanes = slice(block * LANES, (block + 1) * LANES)
             from_lanes = slice(part * SLICE + block * LANES, part * SLICE + (block + 1) * LANES)
             for half, src_ref in enumerate((mine_ref, other_ref)):
                 tiles = []
                 for x in (0, 2):
-                    first = src_ref[quarter, x, :, from_lanes].astype(jnp.float32)
-                    second = src_ref[quarter, x + 1, :, from_lanes].astype(jnp.float32)
+                    first = src_ref[upper, x, :, from_lanes].astype(jnp.float32)
+                    second = src_ref[upper, x + 1, :, from_lanes].astype(jnp.float32)
                     parts = []
                     for q in range(2):
                         one, two = first[q * 8 : q * 8 + 8], second[q * 8 : q * 8 + 8]
@@ -200,19 +200,12 @@
     sin_sum[...] = jnp.zeros_like(sin_sum)
     last_sum[...] = jnp.zeros_like(last_sum)
     steps = FREQS // SLICE
-    cross(0, 0, even_cross)
-
-    def pair(i, carry):
-        cross(i, 1, odd_cross)
-        add(2 * i, even_cross)
-        cross(i + 1, 0, even_cross)
-        add(2 * i + 1, odd_cross)
-        return carry
-
-    lax.fori_loop(0, steps // 2 - 1, pair, 0)
-    cross(steps // 2 - 1, 1, odd_cross)
-    add(steps - 2, even_cross)
-    add(steps - 1, odd_cross)
+    buffers = (even_cross, odd_cross)
+    cross(0, even_cross)
+    for step in range(1, steps):
+        cross(step, buffers[step % 2])
+        add(step - 1, buffers[(step - 1) % 2])
+    add(steps - 1, buffers[(steps - 1) % 2])
 
     period = lax.broadcasted_iota(jnp.int32, (8, LANES), 1) + 1
     wave = unit_circle((period * HALF) & (NSAMP - 1))[0].astype(jnp.bfloat16).astype(jnp.float32)
@@ -251,8 +244,8 @@
 
 
 def body(spectra, dead_mask, seg_offsets, src_index):
-    pos = {axis: lax.axis_index(axis).astype(jnp.int32) for axis in ("y", "h", "x", "c", "n")}
-    wide_pos = ((pos["y"] * 2 + pos["h"]) * 4 + pos["x"]) * 2 + pos["c"]
+    pos = {axis: lax.axis_index(axis).astype(jnp.int32) for axis in ("u", "v", "h", "x", "c", "n")}
+    wide_pos = (((pos["u"] * 2 + pos["v"]) * 2 + pos["h"]) * 4 + pos["x"]) * 2 + pos["c"]
     rows = jnp.transpose(spectra, (2, 1, 0, 3)).reshape(2 * ROWS, SLICE)
     width = src_index.shape[0]
     info = jnp.concatenate(
@@ -271,18 +264,18 @@
         whiten_kernel,
         out_shape=(
             jax.ShapeDtypeStruct((FREQS // SLICE, 2, ROWS, SLICE), jnp.float32),
-            jax.ShapeDtypeStruct((16, QUARTER), jnp.bfloat16),
+            jax.ShapeDtypeStruct((16, SHARE), jnp.bfloat16),
         ),
         in_specs=[smem, vmem],
         out_specs=(vmem, vmem),
-        scratch_shapes=[pltpu.VMEM((4, 2, 16, QUARTER), jnp.float32)],
+        scratch_shapes=[pltpu.VMEM((2, 2, 16, SHARE), jnp.float32)],
         compiler_params=pltpu.CompilerParams(vmem_limit_bytes=32 * 2**20),
         name="whiten",
     )(info, pieces)
 
-    moved = lax.ppermute(src_out, ("y", "h", "n"), scattered())
-    mine = lax.all_to_all(jnp.broadcast_to(moved[None], (16,) + moved.shape), ("y", "x"), 0, 0)
-    mine = mine.reshape((4, 4) + moved.shape)
+    moved = lax.ppermute(src_out, ("u", "v", "h", "n"), scattered())
+    mine = lax.all_to_all(jnp.broadcast_to(moved[None], (8,) + moved.shape), ("v", "x"), 0, 0)
+    mine = mine.reshape((2, 4) + moved.shape)
     other = lax.ppermute(mine, "c", [(0, 1), (1, 0)])
 
     table = pl.pallas_call(
@@ -319,8 +312,8 @@
 
 
 def solution(mesh):
-    parts = Mesh(mesh.devices.reshape(4, 2, 4, 2, 8), ("y", "h", "x", "c", "n"))
-    wide = ("y", "h", "x", "c")
+    parts = Mesh(mesh.devices.reshape(2, 2, 2, 4, 2, 8), ("u", "v", "h", "x", "c", "n"))
+    wide = ("u", "v", "h", "x", "c")
     placed = (P(wide, None, None, "n"), P(wide), P(wide, None), P())
     return jax.shard_map(
         body, mesh=parts, in_specs=placed, out_specs=P("n", wide, None), check_vma=False

time: 66.7 us -> 64.1 us (0.961)
  the two profiles are of different devices: /device:TPU:33 before, /device:TPU:49 now
where the time goes in v5:
time: 64.1 us; the launch traced here: 63.8 us
  starting transfers between devices  29.5 us (46%)
  waiting for transfers between devices  12.4 us (19%)
  blocking collectives  11.4 us (18%)
  Pallas kernels  7.54 us (12%)
  local copies, waits for them, and re-layouts  2.16 us (3%)
  other arithmetic  0.78 us (1%)
    all_to_all x1, starting transfers between devices, body(): lax.all_to_all(jnp.broadcast_to(rows[None], (8, 2 * ROWS, SLICE)), 'n', 0...  12.1 us
    all_to_all x1, blocking collectives, body(): lax.all_to_all(jnp.broadcast_to(moved[None], (8,) + moved.shape), ('v', '...  11.4 us
    ppermute x1, starting transfers between devices, body(): other = lax.ppermute(mine, 'c', [(0, 1), (1, 0)])  10.3 us
    all_to_all x1, waiting for transfers between devices, body(): lax.all_to_all(jnp.broadcast_to(rows[None], (8, 2 * ROWS, SLICE)), 'n', 0...  7.82 us
    ppermute x1, starting transfers between devices, body(): moved = lax.ppermute(src_out, ('u', 'v', 'h', 'n'), scattered())  7.16 us
    ppermute x1, waiting for transfers between devices, body(): moved = lax.ppermute(src_out, ('u', 'v', 'h', 'n'), scattered())  4.53 us
    pallas_call x1, Pallas kernels, body(): pl.pallas_call(correlate_kernel, in_specs=[smem, vmem, vmem, vmem, vmem],...  3.96 us
    pallas_call x1, Pallas kernels, body(): pl.pallas_call(table_kernel, in_specs=[pl.BlockSpec(memory_space=pl.ANY)]...  1.8 us
  transfers between devices with their start and end apart: 3, of which 2 were waited for; matrix products, arithmetic and copies ran while one was open for 2% of the time, Pallas kernels for 3%

profile of v5, /device:TPU:49, one launch (start us, length us, event | category | flops | bytes accessed | tf_op | source)
XLA Modules:
  0.0 63.8 jit_solution(1937451598153668778)
XLA Ops:
  0.0 0.7 %copy.5 = bf16[2,2,6,512]{3,2,1,0:T(8,128)(2,1)S(1)} copy(bf16[2,2,6,512]{3,0,1,2:T(2,128)(2,1)} %bitcast.13) | data formatting | bytes 49152 | tf_op jit(solution)/shard_map/transpose | solution.py:249
  0.8 0.7 %broadcast_in_dim.26 = bf16[8,24,512]{2,1,0:T(8,128)(2,1)} broadcast(bf16[24,512]{1,0:T(8,128)(2,1)S(1)} %broadcast_in_dim.25), dimensions={1,2} | broadcast | bytes 221184 | tf_op jit(solution)/shard_map/broadcast_in_dim | solution.py:259
  1.5 12.1 %all-to-all-start = ((bf16[8,24,512]{2,1,0:T(8,128)(2,1)}), bf16[8,24,512]{2,1,0:T(8,128)(2,1)S(1)}, u32[]{:S(2)}, u32[]{:S(2)}) async-start(bf16[8,24,512]{2,1,0:T(8,128)(2,1)} %broadcast_in_dim.26), calls=%async_computation | async-start | bytes 393216 | tf_op jit(solution)/shard_map/all_to_all | solution.py:259
  13.5 0.1 pad_add_fusion.1
  13.6 0.7 %pad.13 = s32[256]{0:T(256)S(1)} pad(s32[6]{0:T(128)} %param.5, s32[]{:T(128)} %constant.24.clone.1), padding=0_250 | pad | bytes 1052 | tf_op jit(solution)/shard_map/jit(_pad)/pad | solution.py:255
  14.3 0.7 %fusion.1.info_ref = s32[5,256]{1,0:T(8,128)S(1)} fusion(s32[2,6]{1,0:T(2,128)} %bitcast.16, s32[1,256]{1,0:T(1,128)S(1)} %bitcast.14, s32[1,256]{1,0:T(1,128)S(1)} %bitcast.15, s32[1,256]{1,0:T(1,128)} %bitcast.17), kind=kLoop, calls=%fused_computation.2 | loop fusion | flops 3840 | bytes 8240 | tf_op jit(solution)/shard_map/concatenate | solution.py:251
  15.0 7.8 %all-to-all-done.pieces_ref = bf16[8,24,512]{2,1,0:T(8,128)(2,1)S(1)} async-done(((bf16[8,24,512]{2,1,0:T(8,128)(2,1)}), bf16[8,24,512]{2,1,0:T(8,128)(2,1)S(1)}, u32[]{:S(2)}, u32[]{:S(2)}) %all-to-all-start) | async-done | bytes 196640 | tf_op jit(solution)/shard_map/all_to_all | solution.py:259
  22.8 1.8 %whiten.1 = (f32[8,2,12,512]{3,2,1,0:T(8,128)S(1)}, bf16[16,2048]{1,0:T(8,128)(2,1)S(1)}) custom-call(s32[5,256]{1,0:T(8,128)S(1)} %fusion.1.info_ref, bf16[8,24,512]{2,1,0:T(8,128)(2,1)S(1)} %all-to-all-done.pieces_ref), custom_call_target="tpu_custom_call" | custom-call | tf_op jit(solution)/shard_map/whiten/pallas_call | solution.py:263
  24.6 7.2 %collective-permute-start = (bf16[16,2048]{1,0:T(8,128)(2,1)S(1)}, bf16[16,2048]{1,0:T(8,128)(2,1)S(1)}, u32[]{:S(2)}, u32[]{:S(2)}) collective-permute-start(bf16[16,2048]{1,0:T(8,128)(2,1)S(1)} %get-tuple-element.7), channel_id=1, source_target_pairs={{0,256},{1,128},{2,384},{3,0},{4,64},{5,192},{6,448},{7,320},{64,1... | collective-permute-start | bytes 196616 | tf_op jit(solution)/shard_map/ppermute | solution.py:276
  31.8 4.5 %collective-permute-done = bf16[16,2048]{1,0:T(8,128)(2,1)S(1)} collective-permute-done((bf16[16,2048]{1,0:T(8,128)(2,1)S(1)}, bf16[16,2048]{1,0:T(8,128)(2,1)S(1)}, u32[]{:S(2)}, u32[]{:S(2)}) %collective-permute-start) | collective-permute-done | bytes 65568 | tf_op jit(solution)/shard_map/ppermute | solution.py:276
  36.3 11.4 %all_to_all.10 = bf16[8,16,2048]{2,1,0:T(8,128)(2,1)S(1)} all-to-all(bf16[8,16,2048]{2,1,0:T(8,128)(2,1)S(1)} %broadcast_in_dim.27), channel_id=1, replica_groups=mesh['u'=2,'v'=2,'h'=2,'x'=4,'c'=2,'n'=8] {'v','x'}, dimensions={0} | all-to-all | bytes 1048576 | tf_op jit(solution)/shard_map/all_to_all | solution.py:277
  47.7 10.3 %collective-permute-start.1 = (bf16[2,4,16,2048]{3,2,1,0:T(8,128)(2,1)S(1)}, bf16[2,4,16,2048]{3,2,1,0:T(8,128)(2,1)S(1)}, u32[]{:S(2)}, u32[]{:S(2)}) collective-permute-start(bf16[2,4,16,2048]{3,2,1,0:T(8,128)(2,1)S(1)} %bitcast.10), channel_id=1, source_target_pairs={{0,8},{8,0},{1,9},{9,1},{2,10},{10,2},{3,11},{11,3},{4,12},{12,4},... | collective-permute-start | bytes 1572872 | tf_op jit(solution)/shard_map/ppermute | solution.py:279
  58.0 1.8 %lag_table.1.table_ref = bf16[64,64,512]{2,1,0:T(8,128)(2,1)S(1)} custom-call(bf16[2,4,16,2048]{3,2,1,0:T(8,128)(2,1)S(1)} %bitcast.11), custom_call_target="tpu_custom_call" | custom-call | flops 8388608 | bytes 4194304 | tf_op jit(solution)/shard_map/lag_table/pallas_call | solution.py:281
  59.8 0.0 collective-permute-done.1.other_ref
  59.8 4.0 %correlate.1 = f32[6,32,512]{2,1,0:T(8,128)} custom-call(s32[1]{0:T(128)} %bitcast.core_ref, bf16[2,4,16,2048]{3,2,1,0:T(8,128)(2,1)S(1)} %bitcast.12, bf16[2,4,16,2048]{3,2,1,0:T(8,128)(2,1)S(1)} %collective-permute-done.1.other_ref, f32[8,2,12,512]{3,2,1,0:T(8,128)S(1)} %get-tuple-element.8.chan_ref, bf16[64,64,512]{2,1,0:T(8,128)(2,1)S(1)} %lag_table.1.table_ref), custom_call_target="tpu_custom_call" | custom-call | tf_op jit(solution)/shard_map/correlate/pallas_call | solution.py:295
  (3 shorter events, 0.1 us)
Async XLA Ops:
  1.5 21.3 %all-to-all-start = ((bf16[8,24,512]{2,1,0:T(8,128)(2,1)}), bf16[8,24,512]{2,1,0:T(8,128)(2,1)S(1)}, u32[]{:S(2)}, u32[]{:S(2)}) async-start(bf16[8,24,512]{2,1,0:T(8,128)(2,1)} %broadcast_in_dim.26), calls=%async_computation | async-start | bytes 393216 | tf_op jit(solution)/shard_map/all_to_all | solution.py:259
  24.6 11.7 %collective-permute-start = (bf16[16,2048]{1,0:T(8,128)(2,1)S(1)}, bf16[16,2048]{1,0:T(8,128)(2,1)S(1)}, u32[]{:S(2)}, u32[]{:S(2)}) collective-permute-start(bf16[16,2048]{1,0:T(8,128)(2,1)S(1)} %get-tuple-element.7), channel_id=1, source_target_pairs={{0,256},{1,128},{2,384},{3,0},{4,64},{5,192},{6,448},{7,320},{64,1... | collective-permute-start | bytes 196616 | tf_op jit(solution)/shard_map/ppermute | solution.py:276
  47.7 12.1 %collective-permute-start.1 = (bf16[2,4,16,2048]{3,2,1,0:T(8,128)(2,1)S(1)}, bf16[2,4,16,2048]{3,2,1,0:T(8,128)(2,1)S(1)}, u32[]{:S(2)}, u32[]{:S(2)}) collective-permute-start(bf16[2,4,16,2048]{3,2,1,0:T(8,128)(2,1)S(1)} %bitcast.10), channel_id=1, source_target_pairs={{0,8},{8,0},{1,9},{9,1},{2,10},{10,2},{3,11},{11,3},{4,12},{12,4},... | collective-permute-start | bytes 1572872 | tf_op jit(solution)/shard_map/ppermute | solution.py:279

commit v6 on v5

--- a/solution.py
+++ b/solution.py
@@ -45,7 +45,9 @@
 
 def whiten_kernel(info_ref, pieces_ref, chan_ref, src_ref, keep_ref):
     block, place = info_ref[4, 0], info_ref[4, 1]
-    cells = jnp.concatenate([pieces_ref[i] for i in range(FREQS // SLICE)], axis=1).astype(jnp.float32)
+    far = place // 4
+    slices = [pieces_ref[p, (m + far) % 2] for m in range(2) for p in range(4)]
+    cells = jnp.concatenate(slices, axis=1).astype(jnp.float32)
     real, imag = cells[0:ROWS], cells[ROWS : 2 * ROWS]
     amplitude = jnp.sqrt(real * real + imag * imag)
     edge = jnp.zeros((ROWS, LANES), jnp.float32)
@@ -244,7 +246,7 @@
 
 
 def body(spectra, dead_mask, seg_offsets, src_index):
-    pos = {axis: lax.axis_index(axis).astype(jnp.int32) for axis in ("u", "v", "h", "x", "c", "n")}
+    pos = {axis: lax.axis_index(axis).astype(jnp.int32) for axis in ("u", "v", "h", "x", "c", "m", "p")}
     wide_pos = (((pos["u"] * 2 + pos["v"]) * 2 + pos["h"]) * 4 + pos["x"]) * 2 + pos["c"]
     rows = jnp.transpose(spectra, (2, 1, 0, 3)).reshape(2 * ROWS, SLICE)
     width = src_index.shape[0]
@@ -253,10 +255,11 @@
             src_index[None],
             jnp.pad(seg_offsets.T, ((0, 0), (0, width - CH))),
             jnp.pad(dead_mask, (0, width - CH))[None],
-            jnp.pad(jnp.stack([wide_pos, pos["n"]]), (0, width - 2))[None],
+            jnp.pad(jnp.stack([wide_pos, pos["m"] * 4 + pos["p"]]), (0, width - 2))[None],
         ]
     )
-    pieces = lax.all_to_all(jnp.broadcast_to(rows[None], (8, 2 * ROWS, SLICE)), "n", 0, 0)
+    pair = jnp.stack([rows, lax.ppermute(rows, "m", [(0, 1), (1, 0)])])
+    pieces = lax.all_to_all(jnp.broadcast_to(pair[None], (4,) + pair.shape), "p", 0, 0)
 
     vmem = pl.BlockSpec(memory_space=pltpu.VMEM)
     smem = pl.BlockSpec(memory_space=pltpu.SMEM)
@@ -273,7 +276,7 @@
         name="whiten",
     )(info, pieces)
 
-    moved = lax.ppermute(src_out, ("u", "v", "h", "n"), scattered())
+    moved = lax.ppermute(src_out, ("u", "v", "h", "m", "p"), scattered())
     mine = lax.all_to_all(jnp.broadcast_to(moved[None], (8,) + moved.shape), ("v", "x"), 0, 0)
     mine = mine.reshape((2, 4) + moved.shape)
     other = lax.ppermute(mine, "c", [(0, 1), (1, 0)])
@@ -312,9 +315,10 @@
 
 
 def solution(mesh):
-    parts = Mesh(mesh.devices.reshape(2, 2, 2, 4, 2, 8), ("u", "v", "h", "x", "c", "n"))
+    parts = Mesh(mesh.devices.reshape(2, 2, 2, 4, 2, 2, 4), ("u", "v", "h", "x", "c", "m", "p"))
+    line = ("m", "p")
     wide = ("u", "v", "h", "x", "c")
-    placed = (P(wide, None, None, "n"), P(wide), P(wide, None), P())
+    placed = (P(wide, None, None, line), P(wide), P(wide, None), P())
     return jax.shard_map(
-        body, mesh=parts, in_specs=placed, out_specs=P("n", wide, None), check_vma=False
+        body, mesh=parts, in_specs=placed, out_specs=P(line, wide, None), check_vma=False
     )

time: 64.1 us -> 60.8 us (0.949)
  waiting for transfers between devices: 12.4 us -> 7.69 us
  starting transfers between devices: 29.5 us -> 30.3 us
    ppermute x1 -> x2, starting transfers between devices: 7.16 us -> 17.3 us  [the longest x1 8.82 us: body(): pair = jnp.stack([rows, lax.ppermute(rows, 'm', [(0, 1), (1, 0)])])]
    all_to_all x1, starting transfers between devices: 12.1 us -> 5.44 us  [body(): lax.all_to_all(jnp.broadcast_to(pair[None], (4,) + pair.shape), 'p', 0, 0)]
    all_to_all x1, waiting for transfers between devices: 7.82 us -> 3.39 us  [body(): lax.all_to_all(jnp.broadcast_to(pair[None], (4,) + pair.shape), 'p', 0, 0)]
    ppermute x1, starting transfers between devices: 10.3 us -> 7.52 us  [body(): other = lax.ppermute(mine, 'c', [(0, 1), (1, 0)])]
    ppermute x1 -> x2, waiting for transfers between devices: 4.53 us -> 4.3 us  [the longest x1 3.12 us: body(): moved = lax.ppermute(src_out, ('u', 'v', 'h', 'm', 'p'), scattered())]
  transfers between devices with their start and end apart: 3 -> 4, of which waited for: 2 -> 3; matrix products, arithmetic and copies ran while one was open for 2% -> 2% of each run, Pallas kernels for 3% -> 3%
where the time goes in v6:
time: 60.8 us; the launch traced here: 60.4 us
  starting transfers between devices  30.3 us (50%)
  blocking collectives  11.9 us (20%)
  waiting for transfers between devices  7.69 us (13%)
  Pallas kernels  7.57 us (12%)
  local copies, waits for them, and re-layouts  2.18 us (4%)
  other arithmetic  0.79 us (1%)
    all_to_all x1, blocking collectives, body(): lax.all_to_all(jnp.broadcast_to(moved[None], (8,) + moved.shape), ('v', '...  11.9 us
    ppermute x1, starting transfers between devices, body(): pair = jnp.stack([rows, lax.ppermute(rows, 'm', [(0, 1), (1, 0)])])  8.82 us
    ppermute x1, starting transfers between devices, body(): moved = lax.ppermute(src_out, ('u', 'v', 'h', 'm', 'p'), scattered())  8.5 us
    ppermute x1, starting transfers between devices, body(): other = lax.ppermute(mine, 'c', [(0, 1), (1, 0)])  7.52 us
    all_to_all x1, starting transfers between devices, body(): lax.all_to_all(jnp.broadcast_to(pair[None], (4,) + pair.shape), 'p', 0, 0)  5.44 us
    pallas_call x1, Pallas kernels, body(): pl.pallas_call(correlate_kernel, in_specs=[smem, vmem, vmem, vmem, vmem],...  3.96 us
    all_to_all x1, waiting for transfers between devices, body(): lax.all_to_all(jnp.broadcast_to(pair[None], (4,) + pair.shape), 'p', 0, 0)  3.39 us
    ppermute x1, waiting for transfers between devices, body(): moved = lax.ppermute(src_out, ('u', 'v', 'h', 'm', 'p'), scattered())  3.12 us
  transfers between devices with their start and end apart: 4, of which 3 were waited for; matrix products, arithmetic and copies ran while one was open for 2% of the time, Pallas kernels for 3%

profile of v6, /device:TPU:49, one launch (start us, length us, event | category | flops | bytes accessed | tf_op | source)
XLA Modules:
  0.0 60.4 jit_solution(5133048761721119969)
XLA Ops:
  0.0 0.7 %copy.5 = bf16[2,2,6,512]{3,2,1,0:T(8,128)(2,1)S(1)} copy(bf16[2,2,6,512]{3,0,1,2:T(2,128)(2,1)} %bitcast.14) | data formatting | bytes 49152 | tf_op jit(solution)/shard_map/transpose | solution.py:251
  0.8 8.8 %collective-permute-start = (bf16[24,512]{1,0:T(8,128)(2,1)S(1)}, bf16[24,512]{1,0:T(8,128)(2,1)S(1)}, u32[]{:S(2)}, u32[]{:S(2)}) collective-permute-start(bf16[24,512]{1,0:T(8,128)(2,1)S(1)} %reshape.12), channel_id=1, source_target_pairs={{0,4},{4,0},{1,5},{5,1},{2,6},{6,2},{3,7},{7,3},{8,12},{12,8},{9,1... | collective-permute-start | bytes 73736 | tf_op jit(solution)/shard_map/ppermute | solution.py:261
  9.6 1.2 %collective-permute-done = bf16[24,512]{1,0:T(8,128)(2,1)S(1)} collective-permute-done((bf16[24,512]{1,0:T(8,128)(2,1)S(1)}, bf16[24,512]{1,0:T(8,128)(2,1)S(1)}, u32[]{:S(2)}, u32[]{:S(2)}) %collective-permute-start) | collective-permute-done | bytes 24608 | tf_op jit(solution)/shard_map/ppermute | solution.py:261
  10.8 0.7 %broadcast_in_dim.24 = bf16[4,2,24,512]{3,2,1,0:T(8,128)(2,1)} broadcast(bf16[2,24,512]{2,1,0:T(8,128)(2,1)S(1)} %pad_maximum_fusion), dimensions={1,2,3} | broadcast | bytes 245760 | tf_op jit(solution)/shard_map/broadcast_in_dim | solution.py:262
  11.5 5.4 %all-to-all-start = ((bf16[4,2,24,512]{3,2,1,0:T(8,128)(2,1)}), bf16[4,2,24,512]{3,2,1,0:T(8,128)(2,1)S(1)}, u32[]{:S(2)}, u32[]{:S(2)}) async-start(bf16[4,2,24,512]{3,2,1,0:T(8,128)(2,1)} %broadcast_in_dim.24), calls=%async_computation | async-start | bytes 393216 | tf_op jit(solution)/shard_map/all_to_all | solution.py:262
  16.9 0.1 pad_add_fusion.1
  17.0 0.7 %pad.13 = s32[256]{0:T(256)S(1)} pad(s32[6]{0:T(128)} %param.5, s32[]{:T(128)} %constant.26.clone.1), padding=0_250 | pad | bytes 1052 | tf_op jit(solution)/shard_map/jit(_pad)/pad | solution.py:257
  17.7 0.7 %fusion.1.info_ref = s32[5,256]{1,0:T(8,128)S(1)} fusion(s32[2,6]{1,0:T(2,128)} %bitcast.18, s32[1,256]{1,0:T(1,128)S(1)} %bitcast.16, s32[1,256]{1,0:T(1,128)S(1)} %bitcast.17, s32[1,256]{1,0:T(1,128)} %bitcast.19), kind=kLoop, calls=%fused_computation.3 | loop fusion | flops 3840 | bytes 8240 | tf_op jit(solution)/shard_map/concatenate | solution.py:253
  18.4 3.4 %all-to-all-done.pieces_ref = bf16[4,2,24,512]{3,2,1,0:T(8,128)(2,1)S(1)} async-done(((bf16[4,2,24,512]{3,2,1,0:T(8,128)(2,1)}), bf16[4,2,24,512]{3,2,1,0:T(8,128)(2,1)S(1)}, u32[]{:S(2)}, u32[]{:S(2)}) %all-to-all-start) | async-done | bytes 196640 | tf_op jit(solution)/shard_map/all_to_all | solution.py:262
  21.8 1.8 %whiten.1 = (f32[8,2,12,512]{3,2,1,0:T(8,128)S(1)}, bf16[16,2048]{1,0:T(8,128)(2,1)S(1)}) custom-call(s32[5,256]{1,0:T(8,128)S(1)} %fusion.1.info_ref, bf16[4,2,24,512]{3,2,1,0:T(8,128)(2,1)S(1)} %all-to-all-done.pieces_ref), custom_call_target="tpu_custom_call" | custom-call | tf_op jit(solution)/shard_map/whiten/pallas_call | solution.py:266
  23.6 8.5 %collective-permute-start.1 = (bf16[16,2048]{1,0:T(8,128)(2,1)S(1)}, bf16[16,2048]{1,0:T(8,128)(2,1)S(1)}, u32[]{:S(2)}, u32[]{:S(2)}) collective-permute-start(bf16[16,2048]{1,0:T(8,128)(2,1)S(1)} %get-tuple-element.7), channel_id=1, source_target_pairs={{0,256},{1,128},{2,384},{3,0},{4,64},{5,192},{6,448},{7,320},{64,1... | collective-permute-start | bytes 196616 | tf_op jit(solution)/shard_map/ppermute | solution.py:279
  32.1 3.1 %collective-permute-done.1 = bf16[16,2048]{1,0:T(8,128)(2,1)S(1)} collective-permute-done((bf16[16,2048]{1,0:T(8,128)(2,1)S(1)}, bf16[16,2048]{1,0:T(8,128)(2,1)S(1)}, u32[]{:S(2)}, u32[]{:S(2)}) %collective-permute-start.1) | collective-permute-done | bytes 65568 | tf_op jit(solution)/shard_map/ppermute | solution.py:279
  35.3 11.9 %all_to_all.10 = bf16[8,16,2048]{2,1,0:T(8,128)(2,1)S(1)} all-to-all(bf16[8,16,2048]{2,1,0:T(8,128)(2,1)S(1)} %broadcast_in_dim.25), channel_id=1, replica_groups=mesh['u'=2,'v'=2,'h'=2,'x'=4,'c'=2,'m'=2,'p'=4] {'v','x'}, dimensions={0} | all-to-all | bytes 1048576 | tf_op jit(solution)/shard_map/all_to_all | solution.py:280
  47.1 7.5 %collective-permute-start.2 = (bf16[2,4,16,2048]{3,2,1,0:T(8,128)(2,1)S(1)}, bf16[2,4,16,2048]{3,2,1,0:T(8,128)(2,1)S(1)}, u32[]{:S(2)}, u32[]{:S(2)}) collective-permute-start(bf16[2,4,16,2048]{3,2,1,0:T(8,128)(2,1)S(1)} %bitcast.11), channel_id=1, source_target_pairs={{0,8},{8,0},{1,9},{9,1},{2,10},{10,2},{3,11},{11,3},{4,12},{12,4},... | collective-permute-start | bytes 1572872 | tf_op jit(solution)/shard_map/ppermute | solution.py:282
  54.7 1.8 %lag_table.1.table_ref = bf16[64,64,512]{2,1,0:T(8,128)(2,1)S(1)} custom-call(bf16[2,4,16,2048]{3,2,1,0:T(8,128)(2,1)S(1)} %bitcast.12), custom_call_target="tpu_custom_call" | custom-call | flops 8388608 | bytes 4194304 | tf_op jit(solution)/shard_map/lag_table/pallas_call | solution.py:284
  56.5 0.0 collective-permute-done.2.other_ref
  56.5 4.0 %correlate.1 = f32[6,32,512]{2,1,0:T(8,128)} custom-call(s32[1]{0:T(128)} %bitcast.core_ref, bf16[2,4,16,2048]{3,2,1,0:T(8,128)(2,1)S(1)} %bitcast.13, bf16[2,4,16,2048]{3,2,1,0:T(8,128)(2,1)S(1)} %collective-permute-done.2.other_ref, f32[8,2,12,512]{3,2,1,0:T(8,128)S(1)} %get-tuple-element.8.chan_ref, bf16[64,64,512]{2,1,0:T(8,128)(2,1)S(1)} %lag_table.1.table_ref), custom_call_target="tpu_custom_call" | custom-call | tf_op jit(solution)/shard_map/correlate/pallas_call | solution.py:298
  (5 shorter events, 0.1 us)
Async XLA Ops:
  0.8 10.0 %collective-permute-start = (bf16[24,512]{1,0:T(8,128)(2,1)S(1)}, bf16[24,512]{1,0:T(8,128)(2,1)S(1)}, u32[]{:S(2)}, u32[]{:S(2)}) collective-permute-start(bf16[24,512]{1,0:T(8,128)(2,1)S(1)} %reshape.12), channel_id=1, source_target_pairs={{0,4},{4,0},{1,5},{5,1},{2,6},{6,2},{3,7},{7,3},{8,12},{12,8},{9,1... | collective-permute-start | bytes 73736 | tf_op jit(solution)/shard_map/ppermute | solution.py:261
  11.5 10.3 %all-to-all-start = ((bf16[4,2,24,512]{3,2,1,0:T(8,128)(2,1)}), bf16[4,2,24,512]{3,2,1,0:T(8,128)(2,1)S(1)}, u32[]{:S(2)}, u32[]{:S(2)}) async-start(bf16[4,2,24,512]{3,2,1,0:T(8,128)(2,1)} %broadcast_in_dim.24), calls=%async_computation | async-start | bytes 393216 | tf_op jit(solution)/shard_map/all_to_all | solution.py:262
  23.6 11.6 %collective-permute-start.1 = (bf16[16,2048]{1,0:T(8,128)(2,1)S(1)}, bf16[16,2048]{1,0:T(8,128)(2,1)S(1)}, u32[]{:S(2)}, u32[]{:S(2)}) collective-permute-start(bf16[16,2048]{1,0:T(8,128)(2,1)S(1)} %get-tuple-element.7), channel_id=1, source_target_pairs={{0,256},{1,128},{2,384},{3,0},{4,64},{5,192},{6,448},{7,320},{64,1... | collective-permute-start | bytes 196616 | tf_op jit(solution)/shard_map/ppermute | solution.py:279
  47.1 9.3 %collective-permute-start.2 = (bf16[2,4,16,2048]{3,2,1,0:T(8,128)(2,1)S(1)}, bf16[2,4,16,2048]{3,2,1,0:T(8,128)(2,1)S(1)}, u32[]{:S(2)}, u32[]{:S(2)}) collective-permute-start(bf16[2,4,16,2048]{3,2,1,0:T(8,128)(2,1)S(1)} %bitcast.11), channel_id=1, source_target_pairs={{0,8},{8,0},{1,9},{9,1},{2,10},{10,2},{3,11},{11,3},{4,12},{12,4},... | collective-permute-start | bytes 1572872 | tf_op jit(solution)/shard_map/ppermute | solution.py:282

commit v7 on v6

--- a/solution.py
+++ b/solution.py
@@ -248,7 +248,7 @@
 def body(spectra, dead_mask, seg_offsets, src_index):
     pos = {axis: lax.axis_index(axis).astype(jnp.int32) for axis in ("u", "v", "h", "x", "c", "m", "p")}
     wide_pos = (((pos["u"] * 2 + pos["v"]) * 2 + pos["h"]) * 4 + pos["x"]) * 2 + pos["c"]
-    rows = jnp.transpose(spectra, (2, 1, 0, 3)).reshape(2 * ROWS, SLICE)
+    far = lax.ppermute(spectra, "m", [(0, 1), (1, 0)])
     width = src_index.shape[0]
     info = jnp.concatenate(
         [
@@ -258,7 +258,8 @@
             jnp.pad(jnp.stack([wide_pos, pos["m"] * 4 + pos["p"]]), (0, width - 2))[None],
         ]
     )
-    pair = jnp.stack([rows, lax.ppermute(rows, "m", [(0, 1), (1, 0)])])
+    pair = jnp.stack([jnp.transpose(t, (2, 1, 0, 3)).reshape(2 * ROWS, SLICE) for t in (spectra, far)])
+    pair, info = lax.optimization_barrier((pair, info))
     pieces = lax.all_to_all(jnp.broadcast_to(pair[None], (4,) + pair.shape), "p", 0, 0)
 
     vmem = pl.BlockSpec(memory_space=pltpu.VMEM)

time: 60.8 us -> 59.3 us (0.975)
  blocking collectives: 11.9 us -> 21.5 us
  starting transfers between devices: 30.3 us -> 23.6 us
  waiting for transfers between devices: 7.69 us -> 3.84 us
  local copies, waits for them, and re-layouts: 2.18 us -> 1.51 us
    all_to_all x0 -> x1, blocking collectives: none -> 10.1 us  [body(): lax.all_to_all(jnp.broadcast_to(pair[None], (4,) + pair.shape), 'p', 0, 0)]
    all_to_all x1 -> x0, starting transfers between devices: 5.44 us -> none  [body(): lax.all_to_all(jnp.broadcast_to(pair[None], (4,) + pair.shape), 'p', 0, 0)]
    all_to_all x1 -> x0, waiting for transfers between devices: 3.39 us -> none  [body(): lax.all_to_all(jnp.broadcast_to(pair[None], (4,) + pair.shape), 'p', 0, 0)]
    ppermute x1, waiting for transfers between devices: 1.18 us -> 0.01 us  [body(): far = lax.ppermute(spectra, 'm', [(0, 1), (1, 0)])]
    ppermute x1, starting transfers between devices: 8.5 us -> 7.79 us  [body(): moved = lax.ppermute(src_out, ('u', 'v', 'h', 'm', 'p'), scattered())]
    ppermute x1, waiting for transfers between devices: 3.12 us -> 3.83 us  [body(): moved = lax.ppermute(src_out, ('u', 'v', 'h', 'm', 'p'), scattered())]
    broadcast_in_dim x1, local copies, waits for them, and re-layouts: 0.69 us -> 0.01 us  [body(): jnp.broadcast_to(pair[None], (4,) + pair.shape)]
  transfers between devices with their start and end apart: 4 -> 3, of which waited for: 3 -> 1; matrix products, arithmetic and copies ran while one was open for 2% -> 4% of each run, Pallas kernels for 3% -> 3%
where the time goes in v7:
time: 59.3 us; the launch traced here: 59 us
  starting transfers between devices  23.6 us (40%)
  blocking collectives  21.5 us (36%)
  Pallas kernels  7.57 us (13%)
  waiting for transfers between devices  3.84 us (6%)
  local copies, waits for them, and re-layouts  1.51 us (3%)
  other arithmetic  0.79 us (1%)
    all_to_all x1, blocking collectives, body(): lax.all_to_all(jnp.broadcast_to(moved[None], (8,) + moved.shape), ('v', '...  11.5 us
    all_to_all x1, blocking collectives, body(): lax.all_to_all(jnp.broadcast_to(pair[None], (4,) + pair.shape), 'p', 0, 0)  10.1 us
    ppermute x1, starting transfers between devices, body(): far = lax.ppermute(spectra, 'm', [(0, 1), (1, 0)])  8.81 us
    ppermute x1, starting transfers between devices, body(): moved = lax.ppermute(src_out, ('u', 'v', 'h', 'm', 'p'), scattered())  7.79 us
    ppermute x1, starting transfers between devices, body(): other = lax.ppermute(mine, 'c', [(0, 1), (1, 0)])  7.04 us
    pallas_call x1, Pallas kernels, body(): pl.pallas_call(correlate_kernel, in_specs=[smem, vmem, vmem, vmem, vmem],...  3.96 us
    ppermute x1, waiting for transfers between devices, body(): moved = lax.ppermute(src_out, ('u', 'v', 'h', 'm', 'p'), scattered())  3.83 us
    pallas_call x1, Pallas kernels, body(): pl.pallas_call(whiten_kernel, out_shape=(jax.ShapeDtypeStruct((FREQS // S...  1.81 us
  transfers between devices with their start and end apart: 3, of which 1 were waited for; matrix products, arithmetic and copies ran while one was open for 4% of the time, Pallas kernels for 3%

profile of v7, /device:TPU:49, one launch (start us, length us, event | category | flops | bytes accessed | tf_op | source)
XLA Modules:
  0.0 59.0 jit_solution(15581357433314330759)
XLA Ops:
  0.0 8.8 %collective-permute-start = (bf16[6,2,2,512]{3,2,1,0:T(2,128)(2,1)}, bf16[6,2,2,512]{3,2,1,0:T(2,128)(2,1)S(1)}, u32[]{:S(2)}, u32[]{:S(2)}) collective-permute-start(bf16[6,2,2,512]{3,2,1,0:T(2,128)(2,1)} %param.4), channel_id=1, source_target_pairs={{0,4},{4,0},{1,5},{5,1},{2,6},{6,2},{3,7},{7,3},{8,12},{12,8},{9,1... | collective-permute-start | bytes 73736 | tf_op jit(solution)/shard_map/ppermute | solution.py:251
  8.8 0.1 pad_add_fusion.1
  8.9 0.7 %pad.13 = s32[256]{0:T(256)S(1)} pad(s32[6]{0:T(128)} %param.5, s32[]{:T(128)} %constant.26.clone.1), padding=0_250 | pad | bytes 1052 | tf_op jit(solution)/shard_map/jit(_pad)/pad | solution.py:257
  9.6 0.7 %fusion.1.info_ref = s32[5,256]{1,0:T(8,128)S(1)} fusion(s32[2,6]{1,0:T(2,128)} %bitcast.18, s32[1,256]{1,0:T(1,128)S(1)} %bitcast.16, s32[1,256]{1,0:T(1,128)S(1)} %bitcast.17, s32[1,256]{1,0:T(1,128)} %bitcast.19), kind=kLoop, calls=%fused_computation.3 | loop fusion | flops 3840 | bytes 8240 | tf_op jit(solution)/shard_map/concatenate | solution.py:253
  10.3 0.7 %copy.5 = bf16[2,2,6,512]{3,2,1,0:T(8,128)(2,1)S(1)} copy(bf16[2,2,6,512]{3,0,1,2:T(2,128)(2,1)} %bitcast.14) | data formatting | bytes 49152 | tf_op jit(solution)/shard_map/transpose | solution.py:261
  11.1 0.0 collective-permute-done
  11.1 10.1 %all_to_all.10.pieces_ref = bf16[4,2,24,512]{3,2,1,0:T(8,128)(2,1)S(1)} all-to-all(bf16[4,2,24,512]{3,2,1,0:T(8,128)(2,1)S(1)} %broadcast_in_dim.24), channel_id=1, replica_groups=mesh['u'=2,'v'=2,'h'=2,'x'=4,'c'=2,'m'=2,'p'=4] {'p'}, dimensions={0} | all-to-all | bytes 393216 | tf_op jit(solution)/shard_map/all_to_all | solution.py:263
  21.2 1.8 %whiten.1 = (f32[8,2,12,512]{3,2,1,0:T(8,128)S(1)}, bf16[16,2048]{1,0:T(8,128)(2,1)S(1)}) custom-call(s32[5,256]{1,0:T(8,128)S(1)} %fusion.1.info_ref, bf16[4,2,24,512]{3,2,1,0:T(8,128)(2,1)S(1)} %all_to_all.10.pieces_ref), custom_call_target="tpu_custom_call" | custom-call | tf_op jit(solution)/shard_map/whiten/pallas_call | solution.py:267
  23.0 7.8 %collective-permute-start.1 = (bf16[16,2048]{1,0:T(8,128)(2,1)S(1)}, bf16[16,2048]{1,0:T(8,128)(2,1)S(1)}, u32[]{:S(2)}, u32[]{:S(2)}) collective-permute-start(bf16[16,2048]{1,0:T(8,128)(2,1)S(1)} %get-tuple-element.11), channel_id=1, source_target_pairs={{0,256},{1,128},{2,384},{3,0},{4,64},{5,192},{6,448},{7,320},{64,1... | collective-permute-start | bytes 196616 | tf_op jit(solution)/shard_map/ppermute | solution.py:280
  30.8 3.8 %collective-permute-done.1 = bf16[16,2048]{1,0:T(8,128)(2,1)S(1)} collective-permute-done((bf16[16,2048]{1,0:T(8,128)(2,1)S(1)}, bf16[16,2048]{1,0:T(8,128)(2,1)S(1)}, u32[]{:S(2)}, u32[]{:S(2)}) %collective-permute-start.1) | collective-permute-done | bytes 65568 | tf_op jit(solution)/shard_map/ppermute | solution.py:280
  34.7 11.5 %all_to_all.11 = bf16[8,16,2048]{2,1,0:T(8,128)(2,1)S(1)} all-to-all(bf16[8,16,2048]{2,1,0:T(8,128)(2,1)S(1)} %broadcast_in_dim.25), channel_id=1, replica_groups=mesh['u'=2,'v'=2,'h'=2,'x'=4,'c'=2,'m'=2,'p'=4] {'v','x'}, dimensions={0} | all-to-all | bytes 1048576 | tf_op jit(solution)/shard_map/all_to_all | solution.py:281
  46.2 7.0 %collective-permute-start.2 = (bf16[2,4,16,2048]{3,2,1,0:T(8,128)(2,1)S(1)}, bf16[2,4,16,2048]{3,2,1,0:T(8,128)(2,1)S(1)}, u32[]{:S(2)}, u32[]{:S(2)}) collective-permute-start(bf16[2,4,16,2048]{3,2,1,0:T(8,128)(2,1)S(1)} %bitcast.11), channel_id=1, source_target_pairs={{0,8},{8,0},{1,9},{9,1},{2,10},{10,2},{3,11},{11,3},{4,12},{12,4},... | collective-permute-start | bytes 1572872 | tf_op jit(solution)/shard_map/ppermute | solution.py:283
  53.2 1.8 %lag_table.1.table_ref = bf16[64,64,512]{2,1,0:T(8,128)(2,1)S(1)} custom-call(bf16[2,4,16,2048]{3,2,1,0:T(8,128)(2,1)S(1)} %bitcast.12), custom_call_target="tpu_custom_call" | custom-call | flops 8388608 | bytes 4194304 | tf_op jit(solution)/shard_map/lag_table/pallas_call | solution.py:285
  55.0 0.0 collective-permute-done.2.other_ref
  55.1 4.0 %correlate.1 = f32[6,32,512]{2,1,0:T(8,128)} custom-call(s32[1]{0:T(128)} %bitcast.core_ref, bf16[2,4,16,2048]{3,2,1,0:T(8,128)(2,1)S(1)} %bitcast.13, bf16[2,4,16,2048]{3,2,1,0:T(8,128)(2,1)S(1)} %collective-permute-done.2.other_ref, f32[8,2,12,512]{3,2,1,0:T(8,128)S(1)} %get-tuple-element.12.chan_ref, bf16[64,64,512]{2,1,0:T(8,128)(2,1)S(1)} %lag_table.1.table_ref), custom_call_target="tpu_custom_call" | custom-call | tf_op jit(solution)/shard_map/correlate/pallas_call | solution.py:299
  (7 shorter events, 0.1 us)
Async XLA Ops:
  0.0 11.1 %collective-permute-start = (bf16[6,2,2,512]{3,2,1,0:T(2,128)(2,1)}, bf16[6,2,2,512]{3,2,1,0:T(2,128)(2,1)S(1)}, u32[]{:S(2)}, u32[]{:S(2)}) collective-permute-start(bf16[6,2,2,512]{3,2,1,0:T(2,128)(2,1)} %param.4), channel_id=1, source_target_pairs={{0,4},{4,0},{1,5},{5,1},{2,6},{6,2},{3,7},{7,3},{8,12},{12,8},{9,1... | collective-permute-start | bytes 73736 | tf_op jit(solution)/shard_map/ppermute | solution.py:251
  23.0 11.6 %collective-permute-start.1 = (bf16[16,2048]{1,0:T(8,128)(2,1)S(1)}, bf16[16,2048]{1,0:T(8,128)(2,1)S(1)}, u32[]{:S(2)}, u32[]{:S(2)}) collective-permute-start(bf16[16,2048]{1,0:T(8,128)(2,1)S(1)} %get-tuple-element.11), channel_id=1, source_target_pairs={{0,256},{1,128},{2,384},{3,0},{4,64},{5,192},{6,448},{7,320},{64,1... | collective-permute-start | bytes 196616 | tf_op jit(solution)/shard_map/ppermute | solution.py:280
  46.2 8.9 %collective-permute-start.2 = (bf16[2,4,16,2048]{3,2,1,0:T(8,128)(2,1)S(1)}, bf16[2,4,16,2048]{3,2,1,0:T(8,128)(2,1)S(1)}, u32[]{:S(2)}, u32[]{:S(2)}) collective-permute-start(bf16[2,4,16,2048]{3,2,1,0:T(8,128)(2,1)S(1)} %bitcast.11), channel_id=1, source_target_pairs={{0,8},{8,0},{1,9},{9,1},{2,10},{10,2},{3,11},{11,3},{4,12},{12,4},... | collective-permute-start | bytes 1572872 | tf_op jit(solution)/shard_map/ppermute | solution.py:283
